TPU v7x, 512 devices: a whole 4x4x16 slice. The times are simulated.
512 devices in a mesh: pipe: 4 (over z_lo), node: 8 (over z_hi, core), local: 16 (over x, y).
Axes of the slice: x: 4, y: 4, z: 16 (z_hi: 4, z_lo: 4; z = z_hi * 4 + z_lo), core: 2. Of those that a mesh axis runs over, the one named last changes fastest.
Arguments:
- next_grad: bfloat16 [4, 1024, 7168], P('pipe', ('node', 'local')), may hold values from -6 to 6
- routes: int32 [4, 1024, 4], P('pipe', ('node', 'local')), may hold values from 0 to 7, all different within a row; in each aligned block of 8 rows (0 to 7, 8 to 15, ..., all dimensions but the last counted through in order) at most 5 rows name the same one
- probs: bfloat16 [4, 1024, 4], P('pipe', ('node', 'local')), may hold values from 0.099609375 to 1
- down_weight: bfloat16 [4, 8, 2048, 7168], P('pipe', 'node', 'local'), may hold values from -0.0625 to 0.0625
- gate_pre: bfloat16 [4, 8, 640, 2048], P('pipe', 'node', None, 'local'), may hold values from -6 to 6
- up_pre: bfloat16 [4, 8, 640, 2048], P('pipe', 'node', None, 'local'), may hold values from -6 to 6
Outputs:
- gate_grad: bfloat16 [4, 8, 640, 2048], P('pipe', 'node', None, 'local')
- up_grad: bfloat16 [4, 8, 640, 2048], P('pipe', 'node', None, 'local')
- down_grad: bfloat16 [4, 8, 2048, 7168], P('pipe', 'node', 'local')
- prob_grad: float32 [4, 1024, 4], P('pipe', ('node', 'local'))
Inputs may be any that keep to these rules, and one draw needn't show every extreme that they name: `routes`: each row names 4 different nodes; the tokens of one device name one node 5 times at most.
All inputs are finite; a program needn't handle non-finite values.
Results may differ from a plain program's by a relative error of at most 0.0049.
Values may be sent and summed in bfloat16 or wider, within the bound.
A program may use at most 128 MiB of HBM per device.

v0:
```python
import jax
import jax.numpy as jnp
from jax import lax
from jax.sharding import PartitionSpec as P


def from_behind(value, axis, steps):
    count = lax.axis_size(axis)
    pairs = [(source, (source + steps) % count) for source in range(count)]
    return lax.ppermute(value, axis, pairs)


def tables(route_rows, node_count, capacity):
    nodes = jnp.arange(node_count, dtype=jnp.int32)
    node_hits = (route_rows[:, :, None] == nodes[None, None, :]).astype(jnp.int32)
    picked = jnp.sum(node_hits, axis=1)
    earlier = jnp.cumsum(picked, axis=0) - picked
    places = jnp.arange(capacity, dtype=jnp.int32)
    select = (picked.T[:, None, :] == 1) & (earlier.T[:, None, :] == places[None, :, None])
    return (node_hits, select)


def expert_backward(slot_rows, slot_probs, gate_rows, up_rows, weight):
    scores = jnp.einsum("rd,hd->rh", slot_rows, weight, preferred_element_type=jnp.float32)
    gate_value = gate_rows.astype(jnp.float32)
    up_value = up_rows.astype(jnp.float32)
    gate_sig = jax.nn.sigmoid(gate_value)
    activated = gate_value * gate_sig
    hidden = activated * up_value
    partial_value = jnp.sum(hidden * scores, axis=1)
    weights = slot_probs.astype(jnp.float32)[:, None]
    hidden_grad = weights * scores
    d_gate = (hidden_grad * up_value * gate_sig * (1.0 + gate_value * (1.0 - gate_sig))).astype(
        jnp.bfloat16
    )
    d_up = (hidden_grad * activated).astype(jnp.bfloat16)
    scaled_hidden = (weights * hidden).astype(jnp.bfloat16)
    grad_w = jnp.einsum(
        "rh,rd->hd", scaled_hidden, slot_rows, preferred_element_type=jnp.float32
    ).astype(jnp.bfloat16)
    return (partial_value, d_gate, d_up, grad_w)


def reorder(values, first, second, capacity):
    width = values.shape[-1]
    return (
        values.reshape(first, second, capacity, width)
        .transpose(1, 0, 2, 3)
        .reshape(first * second * capacity, width)
    )


def shards(next_grad, routes, probs, down_weight, gate_pre, up_pre):
    node_count = lax.axis_size("node")
    local_count = lax.axis_size("local")
    high = lax.Precision.HIGHEST
    incoming = from_behind(next_grad[0], "pipe", -1)
    route_rows = routes[0]
    prob_rows = probs[0].astype(jnp.float32)
    weight = down_weight[0, 0]
    gate_rows = gate_pre[0, 0]
    up_rows = up_pre[0, 0]
    slot_total = gate_rows.shape[0]
    width = incoming.shape[1]
    capacity = slot_total // (node_count * local_count)
    node_hits, select = tables(route_rows, node_count, capacity)
    select_f = select.astype(jnp.float32)
    send_rows = jnp.einsum(
        "mct,td->mcd", select.astype(jnp.bfloat16), incoming, preferred_element_type=jnp.float32
    ).astype(jnp.bfloat16)
    prob_at = jnp.sum(node_hits.astype(jnp.float32) * prob_rows[:, :, None], axis=1)
    send_probs = jnp.sum(select_f * prob_at.T[:, None, :], axis=2).astype(jnp.bfloat16)
    fanned_rows = jnp.broadcast_to(
        send_rows[:, None], (node_count, local_count, capacity, width)
    ).reshape(node_count * local_count, capacity, width)
    fanned_probs = jnp.broadcast_to(
        send_probs[:, None], (node_count, local_count, capacity)
    ).reshape(node_count * local_count, capacity)
    got_rows, got_probs = (
        lax.all_to_all(fanned_rows, ("node", "local"), split_axis=0, concat_axis=0, tiled=True),
        lax.all_to_all(fanned_probs, ("node", "local"), split_axis=0, concat_axis=0, tiled=True),
    )
    slot_rows = got_rows.reshape(slot_total, width)
    slot_probs = got_probs.reshape(slot_total)
    gate_order = reorder(gate_rows, local_count, node_count, capacity)
    up_order = reorder(up_rows, local_count, node_count, capacity)
    partial_value, gate_moved, up_moved, grad_w = expert_backward(
        slot_rows, slot_probs, gate_order, up_order, weight
    )
    d_gate = reorder(gate_moved, node_count, local_count, capacity)
    d_up = reorder(up_moved, node_count, local_count, capacity)
    sent_back = lax.all_to_all(
        partial_value.reshape(node_count * local_count, capacity),
        ("node", "local"),
        split_axis=0,
        concat_axis=0,
        tiled=True,
    )
    returned = jnp.sum(sent_back.reshape(node_count, local_count, capacity), axis=1)
    value_at = jnp.einsum("mct,mc->tm", select_f, returned, precision=high)
    prob_grad = jnp.einsum("tkm,tm->tk", node_hits.astype(jnp.float32), value_at, precision=high)
    return (d_gate[None, None], d_up[None, None], grad_w[None, None], prob_grad[None])


def solution(mesh):
    return jax.shard_map(
        shards,
        mesh=mesh,
        in_specs=(
            P("pipe", ("node", "local"), None),
            P("pipe", ("node", "local"), None),
            P("pipe", ("node", "local"), None),
            P("pipe", "node", "local", None),
            P("pipe", "node", None, "local"),
            P("pipe", "node", None, "local"),
        ),
        out_specs=(
            P("pipe", "node", None, "local"),
            P("pipe", "node", None, "local"),
            P("pipe", "node", "local", None),
            P("pipe", ("node", "local"), None),
        ),
        check_vma=False,
    )
```

profile of v0, /device:TPU:64, one launch (start us, length us, event | category | flops | bytes accessed | tf_op | source)
XLA Modules:
  0.0 766.0 jit_solution(8747768137320794795)
XLA Ops:
  0.6 0.0 copy-start
  0.6 2.1 collective-permute-start
  2.8 0.8 convert_reduce_fusion
  3.6 0.7 bitcast_convert_fusion
  4.3 0.8 fusion.10
  5.0 0.1 copy.49
  5.1 0.1 copy.48
  5.2 0.1 copy.50
  5.3 0.1 select_reduce_fusion
  5.4 0.1 broadcast_in_dim.8
  5.4 0.1 all_to_all.15
  5.5 0.8 copy.51
  6.3 21.5 %all-to-all-start = ((bf16[128,1,5]{2,1,0:T(2,128)(2,1)}), bf16[128,1,5]{2,1,0:T(2,128)(2,1)S(1)}, u32[]{:S(2)}, u32[]{:S(2)}) async-start(bf16[128,1,5]{2,1,0:T(2,128)(2,1)} %copy.51), calls=%async_computation | async-start | bytes 131072 | tf_op jit(solution)/shard_map/all_to_all | solution.py:81
  27.8 0.0 collective-permute-done
  27.8 0.3 convolution_convert_fusion.1
  28.1 0.3 copy.52
  28.5 16.3 %all-to-all-done = bf16[128,1,5]{2,1,0:T(2,128)(2,1)S(1)} async-done(((bf16[128,1,5]{2,1,0:T(2,128)(2,1)}), bf16[128,1,5]{2,1,0:T(2,128)(2,1)S(1)}, u32[]{:S(2)}, u32[]{:S(2)}) %all-to-all-start) | async-done | bytes 1312 | tf_op jit(solution)/shard_map/all_to_all | solution.py:81
  44.7 7.1 broadcast_in_dim.9
  51.8 0.0 copy-start.3
  51.8 0.0 copy-start.4
  51.8 7.6 all-to-all-start.1
  59.4 0.0 copy-done.3
  59.4 0.1 reshape.92
  59.5 0.8 reshape.87
  60.3 0.0 copy-done.4
  60.3 0.1 reshape.93
  60.4 0.8 reshape.88
  61.2 0.2 convert_reduce_fusion.1
  61.4 0.2 reshape.86
  61.6 0.1 convert_element_type.120
  61.7 0.2 multiply_convert_fusion
  62.0 0.1 convert_element_type.117
  62.1 0.0 copy-start.1
  62.1 0.0 copy-start.2
  62.1 624.1 %all-to-all-done.1 = bf16[128,5,7168]{2,1,0:T(8,128)(2,1)} async-done(((bf16[128,5,7168]{2,1,0:T(8,128)(2,1)}), bf16[128,5,7168]{2,1,0:T(8,128)(2,1)}, u32[]{:S(2)}, u32[]{:S(2)}) %all-to-all-start.1) | async-done | bytes 9175072 | tf_op jit(solution)/shard_map/all_to_all | solution.py:80
  686.2 15.1 %reshape.81 = bf16[640,7168]{1,0:T(8,128)(2,1)} reshape(bf16[128,5,7168]{2,1,0:T(8,128)(2,1)} %all-to-all-done.1) | data formatting | bytes 18350080 | tf_op jit(solution)/shard_map/reshape | solution.py:83
  701.3 0.0 copy-done
  701.3 0.0 copy-done.1
  701.3 0.0 copy-done.2
  701.3 6.2 multiply_reduce_fusion
  707.6 0.0 copy-start.5
  707.6 0.8 all_to_all.18
  708.4 39.9 %all-to-all-start.2 = ((f32[128,1,5]{2,1,0:T(1,128)}), f32[128,1,5]{2,1,0:T(1,128)S(1)}, u32[]{:S(2)}, u32[]{:S(2)}) async-start(f32[128,1,5]{2,1,0:T(1,128)} %bitcast.16), calls=%async_computation.2 | async-start | bytes 131072 | tf_op jit(solution)/shard_map/all_to_all | solution.py:92
  748.3 6.5 fusion
  754.8 0.1 reshape.82
  754.9 0.1 copy.55
  754.9 0.7 broadcast_in_dim_reshape.6
  755.7 0.1 reshape.83
  755.8 0.1 copy.56
  755.8 0.7 broadcast_in_dim_reshape.7
  756.6 8.4 %all-to-all-done.2 = f32[128,1,5]{2,1,0:T(1,128)S(1)} async-done(((f32[128,1,5]{2,1,0:T(1,128)}), f32[128,1,5]{2,1,0:T(1,128)S(1)}, u32[]{:S(2)}, u32[]{:S(2)}) %all-to-all-start.2) | async-done | bytes 2592 | tf_op jit(solution)/shard_map/all_to_all | solution.py:92
  765.0 0.2 fusion.5
  765.2 0.1 copy.68
  765.2 0.0 copy-done.5
  765.2 0.7 fusion.12
  (9 shorter events, 0.2 us)
Async XLA Ops:
  0.6 700.7 %copy-start = (bf16[1,1,128,7168]{3,2,1,0:T(8,128)(2,1)S(1)}, bf16[1,1,128,7168]{3,2,1,0:T(8,128)(2,1)}, u32[]{:S(2)}) copy-start(bf16[1,1,128,7168]{3,2,1,0:T(8,128)(2,1)} %param.9) | copy-start | bytes 5505028
  0.6 27.2 %collective-permute-start = (bf16[8,7168]{1,0:T(8,128)(2,1)}, bf16[8,7168]{1,0:T(8,128)(2,1)S(1)}, u32[]{:S(2)}, u32[]{:S(2)}) collective-permute-start(bf16[8,7168]{1,0:T(8,128)(2,1)} %bitcast.70), channel_id=1, source_target_pairs={{0,384},{128,0},{256,128},{384,256},{1,385},{129,1},{257,129},{385... | collective-permute-start | bytes 344072 | tf_op jit(solution)/shard_map/ppermute | solution.py:10
  6.3 38.4 %all-to-all-start = ((bf16[128,1,5]{2,1,0:T(2,128)(2,1)}), bf16[128,1,5]{2,1,0:T(2,128)(2,1)S(1)}, u32[]{:S(2)}, u32[]{:S(2)}) async-start(bf16[128,1,5]{2,1,0:T(2,128)(2,1)} %copy.51), calls=%async_computation | async-start | bytes 131072 | tf_op jit(solution)/shard_map/all_to_all | solution.py:81
  51.8 7.6 copy-start.3
  51.8 8.5 %copy-start.4 = (bf16[1,1,640,128]{3,2,1,0:T(8,128)(2,1)S(1)}, bf16[1,1,640,128]{3,2,1,0:T(8,128)(2,1)}, u32[]{:S(2)}) copy-start(bf16[1,1,640,128]{3,2,1,0:T(8,128)(2,1)} %param.10) | copy-start | bytes 491524
  51.8 634.4 %all-to-all-start.1 = ((bf16[128,5,7168]{2,1,0:T(8,128)(2,1)}), bf16[128,5,7168]{2,1,0:T(8,128)(2,1)}, u32[]{:S(2)}, u32[]{:S(2)}) async-start(bf16[128,5,7168]{2,1,0:T(8,128)(2,1)} %bitcast.56), calls=%async_computation.1 | async-start | bytes 29360128 | tf_op jit(solution)/shard_map/all_to_all | solution.py:80
  62.1 639.2 %copy-start.1 = (f32[640,128]{1,0:T(8,128)S(1)}, f32[640,128]{1,0:T(8,128)}, u32[]{:S(2)}) copy-start(f32[640,128]{1,0:T(8,128)} %reshape.87) | copy-start | bytes 983044
  62.1 639.2 %copy-start.2 = (f32[640,128]{1,0:T(8,128)S(1)}, f32[640,128]{1,0:T(8,128)}, u32[]{:S(2)}) copy-start(f32[640,128]{1,0:T(8,128)} %reshape.88) | copy-start | bytes 983044
  707.6 57.7 %copy-start.5 = (s32[1,8,4]{1,2,0:T(4,128)S(1)}, s32[1,8,4]{1,2,0:T(4,128)}, u32[]{:S(2)}) copy-start(s32[1,8,4]{1,2,0:T(4,128)} %param.7) | copy-start | bytes 388
  708.4 56.6 %all-to-all-start.2 = ((f32[128,1,5]{2,1,0:T(1,128)}), f32[128,1,5]{2,1,0:T(1,128)S(1)}, u32[]{:S(2)}, u32[]{:S(2)}) async-start(f32[128,1,5]{2,1,0:T(1,128)} %bitcast.16), calls=%async_computation.2 | async-start | bytes 131072 | tf_op jit(solution)/shard_map/all_to_all | solution.py:92
where the time goes:
time: 767 us; the launch traced here: 766 us
  waiting for transfers between devices  649 us (85%)
  starting transfers between devices  71.2 us (9%)
  local copies, waits for them, and re-layouts  28.4 us (4%)
  matrix products  13.2 us (2%)
    all_to_all x1, waiting for transfers between devices, shards(): lax.all_to_all(fanned_rows, ('node', 'local'), split_axis=0, concat_axis=...  624 us
    all_to_all x1, starting transfers between devices, shards(): lax.all_to_all(partial_value.reshape(node_count * local_count, capacity),...  39.9 us
    all_to_all x1, starting transfers between devices, shards(): lax.all_to_all(fanned_probs, ('node', 'local'), split_axis=0, concat_axis...  21.5 us
    all_to_all x1, waiting for transfers between devices, shards(): lax.all_to_all(fanned_probs, ('node', 'local'), split_axis=0, concat_axis...  16.3 us
  transfers between devices with their start and end apart: 4, of which 3 were waited for; matrix products, arithmetic and copies ran while one was open for 2% of the time, Pallas kernels for 0%

commit v1 on v0

v1 whole, which is shorter than its diff:
```python
import functools

import jax
import jax.numpy as jnp
from jax import lax
from jax.experimental import pallas as pl
from jax.experimental.pallas import tpu as pltpu
from jax.sharding import PartitionSpec as P

MESH = pl.DeviceIdType.MESH
F32 = jnp.float32
BF16 = jnp.bfloat16
SIDE = 4
CAP = 5
TOK = 8
ROWS = 16
NT = (((1,), (1,)), ((), ()))


def kernel(
    sections,
    grad_ref,
    routes_ref,
    probs_ref,
    weight_hbm,
    gate_hbm,
    up_hbm,
    gate_out,
    up_out,
    down_out,
    prob_out,
    rows_buf,
    own_buf,
    weight_buf,
    pre_buf,
    pre_t,
    meta1,
    meta2,
    select,
    hid,
    gate_f,
    up_f,
    scaled,
    total,
    slot_total,
    slot_out,
    down_buf,
    part_send,
    part_recv,
    part2,
    z_recv,
    s1_recv,
    s2_recv,
    s3_recv,
    s4_recv,
    sib_recv,
    z_send,
    s1_send,
    s2_send,
    s3_send,
    s4_send,
    sib_send,
    meta_send,
    meta_recv,
    part_ssem,
    part_rsem,
    load_sem,
    store_sem,
):
    half = rows_buf.shape[-1]
    mid = half // 2
    quarter = mid // 2
    s = lax.axis_index("pipe")
    node = lax.axis_index("node")
    local = lax.axis_index("local")
    h, k = node // 2, lax.rem(node, 2)
    x, y = local // SIDE, lax.rem(local, SIDE)

    def ring(value):
        return lax.rem(value + 2 * SIDE, SIDE)

    def at(section, plane, core, px, py):
        return {"pipe": section, "node": plane * 2 + core, "local": px * SIDE + py}

    def remote(src, dst, ssem, rsem, device):
        return pltpu.make_async_remote_copy(
            src_ref=src, dst_ref=dst, send_sem=ssem, recv_sem=rsem, device_id=device, device_id_type=MESH
        )

    def send(ref, ssem, rsem, device):
        remote(ref, ref, ssem, rsem, device).start()

    def drain(ref, sem):
        pltpu.make_async_copy(ref, ref, sem).wait()

    s_up = lax.rem(s + 1, sections)
    s_down = lax.rem(s + sections - 1, sections)
    h_first = ring(h + jnp.where(s == sections - 1, 1, 0))
    h_back = ring(h - jnp.where(s == 0, 1, 0))

    line = y * 2 + k
    grid = h * SIDE + x

    def line_peer(j):
        other = lax.rem(line + j, 2 * SIDE)
        return at(s, h, lax.rem(other, 2), x, other // 2)

    def grid_peer(j):
        other = lax.rem(grid + j, SIDE * SIDE)
        return at(s, other // SIDE, k, lax.rem(other, SIDE), y)

    loads = [
        pltpu.make_async_copy(gate_hbm, pre_buf.at[0], load_sem.at[0]),
        pltpu.make_async_copy(up_hbm, pre_buf.at[1], load_sem.at[1]),
        pltpu.make_async_copy(weight_hbm.at[:, 0:half], weight_buf.at[0:128], load_sem.at[2]),
        pltpu.make_async_copy(weight_hbm.at[:, half : 2 * half], weight_buf.at[128:256], load_sem.at[3]),
    ]
    for load in loads:
        load.start()

    barrier = pltpu.get_barrier_semaphore()

    def greet(device):
        pl.semaphore_signal(barrier, inc=1, device_id=device, device_id_type=MESH)

    greet(at(s_up, h_first, k, x, y))
    greet(at(s_up, ring(h_first - 1), k, x, y))

    @pl.loop(1, 2 * SIDE)
    def _(j):
        greet(line_peer(j))

    @pl.loop(1, SIDE * SIDE)
    def _(j):
        greet(grid_peer(j))

    own_buf[0:TOK, :] = grad_ref[:, 0:half]
    own_buf[TOK:ROWS, :] = grad_ref[:, half : 2 * half]

    route_rows = routes_ref[...]
    prob_rows = probs_ref[...].astype(F32)
    lane = lax.broadcasted_iota(jnp.int32, (TOK, 128), 1)
    token = lax.broadcasted_iota(jnp.int32, (TOK, 128), 0)
    mine = lane - (y * 32 + k * ROWS) == token
    row16 = lax.broadcasted_iota(jnp.int32, (ROWS, 128), 0)
    tile = jnp.zeros((ROWS, 128), F32)
    for m in range(2 * SIDE):
        column = jnp.sum(jnp.where(route_rows == m, prob_rows, 0.0), axis=1, keepdims=True)
        row = jnp.sum(jnp.where(mine, column, 0.0), axis=0, keepdims=True)
        tile = tile + jnp.where(row16 == m, row, 0.0)
    meta1[line] = tile.astype(BF16)

    pl.semaphore_wait(barrier, 2 + (2 * SIDE - 1) + (SIDE * SIDE - 1))

    def z_copy(src, wave, hsrc, section, plane):
        return remote(
            src, rows_buf.at[hsrc, x, y, k], z_send.at[wave], z_recv.at[wave], at(section, plane, k, x, y)
        )

    z_copy(own_buf, 0, h, s_down, h_back).start()
    z_copy(own_buf, 1, h, s_down, ring(h_back + 1)).start()

    @pl.loop(1, 2 * SIDE)
    def _(j):
        send(meta1.at[line], meta_send.at[0], meta_recv.at[0], line_peer(j))

    def source(wave):
        return lax.rem(h_first + SIDE - wave, SIDE)

    def z_wait(wave):
        hw = source(wave)
        drain(rows_buf.at[hw, x, y, k], z_recv.at[wave])

    left, right = (0, mid), (mid, mid)

    def part(cols, piece):
        return pl.ds(cols[0] + piece * quarter, quarter)

    def row_blk(hw, px, cols):
        return rows_buf.at[hw, px, y, k, :, cols]

    def col_blk(hw, py, cols):
        return rows_buf.at[hw, x, py, k, :, cols]

    def row_set(hw, py, core, cols):
        return rows_buf.at[hw, :, py, core, :, cols]

    def col_set(hw, px, core, cols):
        return rows_buf.at[hw, px, :, core, :, cols]

    lcols, rcols = pl.ds(*left), pl.ds(*right)
    x_up, x_down, x_far = ring(x + 1), ring(x - 1), ring(x + 2)
    y_up, y_down, y_far = ring(y + 1), ring(y - 1), ring(y + 2)
    dev_x = (at(s, h, k, x_up, y), at(s, h, k, x_down, y))
    dev_y = (at(s, h, k, x, y_up), at(s, h, k, x, y_down))
    sibling = at(s, h, 1 - k, x, y)
    from_x, from_y = (x_down, x_up), (y_down, y_up)

    def step1(w):
        hw = source(w)
        for d in range(2):
            send(row_blk(hw, x, lcols), s1_send.at[w], s1_recv.at[w, d], dev_x[d])
            send(col_blk(hw, y, rcols), s1_send.at[w], s1_recv.at[w, 2 + d], dev_y[d])

    def step2(w):
        hw = source(w)
        for d in range(2):
            drain(row_blk(hw, from_x[d], lcols), s1_recv.at[w, d])
            send(row_blk(hw, from_x[d], part(left, d)), s2_send.at[w], s2_recv.at[w, 0], dev_x[d])
            drain(col_blk(hw, from_y[d], rcols), s1_recv.at[w, 2 + d])
            send(col_blk(hw, from_y[d], part(right, d)), s2_send.at[w], s2_recv.at[w, 1], dev_y[d])

    def step3(w):
        hw = source(w)
        drain(row_blk(hw, x_far, lcols), s2_recv.at[w, 0])
        for d in range(2):
            send(row_set(hw, y, k, lcols), s3_send.at[w], s3_recv.at[w, d], dev_y[d])
        drain(col_blk(hw, y_far, rcols), s2_recv.at[w, 1])
        for d in range(2):
            send(col_set(hw, x, k, rcols), s3_send.at[w], s3_recv.at[w, 2 + d], dev_x[d])
        hand(row_set(hw, y, k, lcols), w)
        hand(col_set(hw, x, k, rcols), w)

    def hand(ref, w):
        send(ref, sib_send.at[w], sib_recv.at[w], sibling)

    def step4(w):
        hw = source(w)
        for d in range(2):
            drain(row_set(hw, from_y[d], k, lcols), s3_recv.at[w, d])
            send(row_set(hw, from_y[d], k, part(left, d)), s4_send.at[w], s4_recv.at[w, 0], dev_y[d])
            drain(col_set(hw, from_x[d], k, rcols), s3_recv.at[w, 2 + d])
            send(col_set(hw, from_x[d], k, part(right, d)), s4_send.at[w], s4_recv.at[w, 1], dev_x[d])
        for d in range(2):
            hand(row_set(hw, from_y[d], k, lcols), w)
            hand(col_set(hw, from_x[d], k, rcols), w)

    def step5(w):
        hw = source(w)
        drain(row_set(hw, y_far, k, lcols), s4_recv.at[w, 0])
        hand(row_set(hw, y_far, k, lcols), w)
        drain(col_set(hw, x_far, k, rcols), s4_recv.at[w, 1])
        hand(col_set(hw, x_far, k, rcols), w)

    def arrived(w):
        drain(rows_buf.at[source(w), :, :, 1 - k], sib_recv.at[w])

    def sent(w):
        drain(rows_buf.at[0, 0, 0:2, 0], s1_send.at[w])
        drain(rows_buf.at[0, 0, 0, 0], s2_send.at[w])
        drain(rows_buf.at[0, 0:2, :, 0], s3_send.at[w])
        drain(rows_buf.at[0, 0, :, 0], s4_send.at[w])
        drain(rows_buf.at[0, :, :, 0], sib_send.at[w])

    z_wait(0)
    z_copy(rows_buf.at[h_first, x, y, k], 3, h_first, s, ring(h - 1)).start()
    step1(0)

    drain(meta1.at[0 : 2 * SIDE - 1], meta_recv.at[0])
    meta2[grid] = jnp.sum(meta1[...].astype(F32), axis=0).astype(BF16)

    @pl.loop(1, SIDE * SIDE)
    def _(j):
        send(meta2.at[grid], meta_send.at[1], meta_recv.at[1], grid_peer(j))

    step2(0)
    z_wait(1)
    z_copy(rows_buf.at[source(1), x, y, k], 2, source(1), s, ring(h + 1)).start()
    step3(0)
    step1(1)

    drain(meta2.at[0 : SIDE * SIDE - 1], meta_recv.at[1])
    for load in loads:
        load.wait()
    pre_t[...] = jnp.concatenate([pre_buf[0], pre_buf[1]], axis=1).astype(F32).T.astype(BF16)
    tokens = SIDE * 128
    slots = slot_total.shape[0]

    @pl.loop(0, SIDE)
    def _(hw):
        tiles = jnp.concatenate([meta2[hw * SIDE + j] for j in range(SIDE)], axis=1).astype(F32)
        rows = lax.broadcasted_iota(jnp.int32, (ROWS, tokens), 0)
        prob = jnp.sum(jnp.where(rows == node, tiles, 0.0), axis=0, keepdims=True)
        prob8 = jnp.broadcast_to(prob, (8, tokens))
        hit = jnp.where(prob8 > 0.0, 1.0, 0.0)
        at_lane = lax.broadcasted_iota(jnp.int32, (8, tokens), 1)
        place = lax.rem(at_lane, ROWS)
        rank = jnp.zeros((8, tokens), F32)
        for back in range(1, TOK):
            rank = rank + jnp.where(place >= back, pltpu.roll(hit, back, axis=1), 0.0)
        group = (at_lane // 32) * (2 * SIDE) + 2 * hw + lax.rem(at_lane // ROWS, 2)
        slot = jnp.where(prob8 > 0.0, group * CAP + rank.astype(jnp.int32), -1)[0:1]
        slot_row = lax.broadcasted_iota(jnp.int32, (slots, tokens), 0)
        select[hw] = jnp.where(slot_row == slot, 1.0, 0.0).astype(BF16)
        moved = jnp.dot(pre_t[...], select[hw], preferred_element_type=F32)
        gate, up = moved[0:128], moved[128:256]
        sig = 1.0 / (1.0 + jnp.exp(-gate))
        act = gate * sig
        hidden = act * up
        hid[hw] = hidden
        gate_f[hw] = prob * (up * sig * (1.0 + gate * (1.0 - sig)))
        up_f[hw] = prob * act
        scaled_hidden = prob * hidden
        scaled[hw, 0:128] = scaled_hidden.astype(BF16)
        scaled[hw, 128:256] = pltpu.roll(scaled_hidden, TOK, axis=1).astype(BF16)

    def compute(w):
        hw = source(w)

        @pl.loop(0, 2)
        def _(j):
            block = rows_buf[hw, pl.ds(2 * j, 2)].reshape(256, half)
            both = lax.dot_general(weight_buf[...], block, NT, preferred_element_type=F32)
            scores = both[0:128] + pltpu.roll(both[128:256], 256 - TOK, axis=1)
            cols = pl.ds(pl.multiple_of(j * 256, 256), 256)
            shares = jnp.sum((hid[hw, :, cols] * scores).reshape(ROWS, 8, 256), axis=0)
            part_send[hw, 2 * j] = shares[:, 0:128]
            part_send[hw, 2 * j + 1] = shares[:, 128:256]
            d_gate = (gate_f[hw, :, cols] * scores).astype(BF16)
            d_up = (up_f[hw, :, cols] * scores).astype(BF16)
            moved = lax.dot_general(
                select[hw, :, cols], jnp.concatenate([d_gate, d_up], axis=0), NT, preferred_element_type=F32
            )
            first = (w == 0) & (j == 0)

            @pl.when(first)
            def _():
                slot_total[...] = moved

            @pl.when(jnp.logical_not(first))
            def _():
                slot_total[...] += moved

        @pl.loop(0, SIDE)
        def _(px):
            own = (hw == h) & (px == x)

            @pl.when(own)
            def _():
                part_recv[grid] = part_send[hw, px]

            @pl.when(jnp.logical_not(own))
            def _():
                remote(
                    part_send.at[hw, px], part_recv.at[grid], part_ssem.at[0], part_rsem.at[0], at(s, hw, k, px, y)
                ).start()

        @pl.loop(0, half // 512)
        def _(c):
            cols = pl.ds(pl.multiple_of(c * 512, 512), 512)
            block = rows_buf[hw, :, :, :, :, cols].reshape(tokens, 512)
            more = jnp.dot(scaled[hw], block, preferred_element_type=F32)

            @pl.when(w == 0)
            def _():
                total[:, cols] = more

            @pl.when((w > 0) & (w < SIDE - 1))
            def _():
                total[:, cols] += more

            @pl.when(w == SIDE - 1)
            def _():
                down_buf[:, cols] = (total[:, cols] + more).astype(BF16)

    @pl.loop(0, SIDE + 1)
    def _(w):
        @pl.when(w > 0)
        def _():
            compute(w - 1)

        @pl.when(w < SIDE)
        def _():
            step4(w)

            @pl.when(w < SIDE - 1)
            def _():
                step2(w + 1)
                step3(w + 1)

            @pl.when(w < SIDE - 2)
            def _():
                z_wait(w + 2)
                step1(w + 2)

            step5(w)
            arrived(w)

    stores = [
        pltpu.make_async_copy(down_buf.at[0:128], down_out.at[:, 0:half], store_sem.at[0]),
        pltpu.make_async_copy(down_buf.at[128:256], down_out.at[:, half : 2 * half], store_sem.at[1]),
        pltpu.make_async_copy(slot_out.at[0], gate_out, store_sem.at[2]),
        pltpu.make_async_copy(slot_out.at[1], up_out, store_sem.at[3]),
    ]
    stores[0].start()
    stores[1].start()
    slot_out[0] = slot_total[:, 0:128].astype(BF16)
    slot_out[1] = slot_total[:, 128:256].astype(BF16)
    stores[2].start()
    stores[3].start()

    drain(part_recv.at[0 : SIDE * SIDE - 1], part_rsem.at[0])
    row8 = lax.broadcasted_iota(jnp.int32, (8, 128), 0)
    tile = jnp.zeros((8, 128), F32)
    for plane in range(SIDE):
        over_x = part_recv[plane * SIDE]
        for px in range(1, SIDE):
            over_x = over_x + part_recv[plane * SIDE + px]
        tile = tile + jnp.where(row8 == plane, jnp.sum(over_x, axis=0, keepdims=True), 0.0)
    part2[line] = tile

    @pl.loop(1, 2 * SIDE)
    def _(j):
        send(part2.at[line], part_ssem.at[1], part_rsem.at[1], line_peer(j))

    @pl.loop(0, SIDE)
    def _(w):
        sent(w)
        drain(rows_buf.at[0, 0, 0, 0], z_send.at[w])

    drain(meta1.at[0 : 2 * SIDE - 1], meta_send.at[0])
    drain(meta2.at[0 : SIDE * SIDE - 1], meta_send.at[1])
    drain(part_recv.at[0 : SIDE * SIDE - 1], part_ssem.at[0])

    drain(part2.at[0 : 2 * SIDE - 1], part_rsem.at[1])
    result = jnp.zeros((TOK, routes_ref.shape[1]), F32)
    for core in range(2):
        over_y = part2[core]
        for py in range(1, SIDE):
            over_y = over_y + part2[py * 2 + core]
        for plane in range(SIDE):
            column = jnp.sum(jnp.where(mine, over_y[plane : plane + 1], 0.0), axis=1, keepdims=True)
            result = result + jnp.where(route_rows == plane * 2 + core, column, 0.0)
    prob_out[...] = result
    drain(part2.at[0 : 2 * SIDE - 1], part_ssem.at[1])
    for store in stores:
        store.wait()


def shards(next_grad, routes, probs, down_weight, gate_pre, up_pre):
    sections = lax.axis_size("pipe")
    grad = next_grad[0]
    weight = down_weight[0, 0]
    gate_rows = gate_pre[0, 0]
    slots, hidden = gate_rows.shape
    width = grad.shape[1]
    half = width // 2
    tokens = SIDE * 128
    vmem = pl.BlockSpec(memory_space=pltpu.VMEM)
    hbm = pl.BlockSpec(memory_space=pl.ANY)
    dma = pltpu.SemaphoreType.DMA
    gate_grad, up_grad, down_grad, prob_grad = pl.pallas_call(
        functools.partial(kernel, sections),
        out_shape=(
            jax.ShapeDtypeStruct((slots, hidden), BF16),
            jax.ShapeDtypeStruct((slots, hidden), BF16),
            jax.ShapeDtypeStruct((hidden, width), BF16),
            jax.ShapeDtypeStruct(routes.shape[1:], F32),
        ),
        in_specs=[vmem, vmem, vmem, hbm, hbm, hbm],
        out_specs=(hbm, hbm, hbm, vmem),
        scratch_shapes=[
            pltpu.VMEM((SIDE, SIDE, SIDE, 2, ROWS, half), BF16),
            pltpu.VMEM((ROWS, half), BF16),
            pltpu.VMEM((2 * hidden, half), BF16),
            pltpu.VMEM((2, slots, hidden), BF16),
            pltpu.VMEM((2 * hidden, slots), BF16),
            pltpu.VMEM((2 * SIDE, ROWS, 128), BF16),
            pltpu.VMEM((SIDE * SIDE, ROWS, 128), BF16),
            pltpu.VMEM((SIDE, slots, tokens), BF16),
            pltpu.VMEM((SIDE, hidden, tokens), F32),
            pltpu.VMEM((SIDE, hidden, tokens), F32),
            pltpu.VMEM((SIDE, hidden, tokens), F32),
            pltpu.VMEM((SIDE, 2 * hidden, tokens), BF16),
            pltpu.VMEM((2 * hidden, half), F32),
            pltpu.VMEM((slots, 2 * hidden), F32),
            pltpu.VMEM((2, slots, hidden), BF16),
            pltpu.VMEM((2 * hidden, half), BF16),
            pltpu.VMEM((SIDE, SIDE, 8, 128), F32),
            pltpu.VMEM((SIDE * SIDE, 8, 128), F32),
            pltpu.VMEM((2 * SIDE, 8, 128), F32),
            dma((SIDE,)),
            dma((SIDE, 4)),
            dma((SIDE, 2)),
            dma((SIDE, 4)),
            dma((SIDE, 2)),
            dma((SIDE,)),
            dma((SIDE,)),
            dma((SIDE,)),
            dma((SIDE,)),
            dma((SIDE,)),
            dma((SIDE,)),
            dma((SIDE,)),
            dma((2,)),
            dma((2,)),
            dma((2,)),
            dma((2,)),
            dma((4,)),
            dma((4,)),
        ],
        compiler_params=pltpu.CompilerParams(
            collective_id=0, has_side_effects=True, vmem_limit_bytes=56 * 1024 * 1024
        ),
        cost_estimate=pl.CostEstimate(
            flops=4 * slots * hidden * width, bytes_accessed=4 * hidden * width, transcendentals=slots * hidden
        ),
    )(grad, routes[0], probs[0], weight, gate_rows, up_pre[0, 0])
    return (gate_grad[None, None], up_grad[None, None], down_grad[None, None], prob_grad[None])


def solution(mesh):
    return jax.shard_map(
        shards,
        mesh=mesh,
        in_specs=(
            P("pipe", ("node", "local"), None),
            P("pipe", ("node", "local"), None),
            P("pipe", ("node", "local"), None),
            P("pipe", "node", "local", None),
            P("pipe", "node", None, "local"),
            P("pipe", "node", None, "local"),
        ),
        out_specs=(
            P("pipe", "node", None, "local"),
            P("pipe", "node", None, "local"),
            P("pipe", "node", "local", None),
            P("pipe", ("node", "local"), None),
        ),
        check_vma=False,
    )
```

time: 767 us -> 111 us (0.14)
  waiting for transfers between devices: 649 us -> 0 us
  Pallas kernels: 0 us -> 99.8 us
  starting transfers between devices: 71.2 us -> 0 us
  local copies, waits for them, and re-layouts: 28.4 us -> 10 us
  matrix products: 13.2 us -> 0 us
    all_to_all x3 -> x0, waiting for transfers between devices: 649 us -> none  [the longest x1 624 us: shards(): lax.all_to_all(fanned_rows, ('node', 'local'), split_axis=0, concat_axis=...]
    pallas_call x0 -> x1, Pallas kernels: none -> 99.8 us  [shards(): pl.pallas_call(functools.partial(kernel, sections), out_shape=(jax.ShapeD...]
    all_to_all x3 -> x0, starting transfers between devices: 69 us -> none  [the longest x1 39.9 us: shards(): lax.all_to_all(partial_value.reshape(node_count * local_count, capacity),...]
    reshape x3 -> x0, local copies, waits for them, and re-layouts: 15.2 us -> none  [the longest x1 15.1 us: shards(): slot_rows = got_rows.reshape(slot_total, width)]
    dot_general x4 -> x0, matrix products: 13.2 us -> none  [the longest x1 6.48 us: expert_backward(): jnp.einsum('rh,rd->hd', scaled_hidden, slot_rows, preferred_element_type=...]
  transfers between devices with their start and end apart: 4 -> 0, of which waited for: 3 -> 0; matrix products, arithmetic and copies ran while one was open for 2% -> 0% of each run, Pallas kernels for 0% -> 0%
where the time goes in v1:
time: 111 us
  Pallas kernels  99.8 us (90%)
  local copies, waits for them, and re-layouts  10 us (9%)
    pallas_call x1, Pallas kernels, shards(): pl.pallas_call(functools.partial(kernel, sections), out_shape=(jax.ShapeD...  99.8 us
    unnamed x3, local copies, waits for them, and re-layouts  6.03 us

profile of v1, /device:TPU:64, one launch (start us, length us, event | category | flops | bytes accessed | tf_op | source)
XLA Modules:
  0.0 110.5 jit_solution(1593906951228043557)
XLA Ops:
  0.6 1.3 %copy.11.probs_ref = bf16[8,4]{1,0:T(8,128)(2,1)} copy(bf16[8,4]{0,1:T(4,128)(2,1)} %bitcast.15) | data formatting | bytes 128 | tf_op jit(solution)/shard_map/squeeze | solution.py:507
  2.0 1.3 %copy.10.routes_ref = s32[8,4]{1,0:T(8,128)} copy(s32[8,4]{0,1:T(4,128)} %bitcast.13) | data formatting | bytes 256 | tf_op jit(solution)/shard_map/squeeze | solution.py:507
  3.3 99.8 %shard_map.93 = (bf16[640,128]{1,0:T(8,128)(2,1)}, bf16[640,128]{1,0:T(8,128)(2,1)}, bf16[128,7168]{1,0:T(8,128)(2,1)}, f32[8,4]{1,0:T(8,128)}) custom-call(bf16[8,7168]{1,0:T(8,128)(2,1)} %bitcast.19, s32[8,4]{1,0:T(8,128)} %copy.10.routes_ref, bf16[8,4]{1,0:T(8,128)(2,1)} %copy.11.probs_ref, bf16[128,7168]{1,0:T(8,128)(2,1)} %bitcast.16, ...), custom_call_target="tpu_custom_call" | custom-call | flops 2348810240 | bytes 3670016 | tf_op jit(solution)/shard_map/pallas_call | solution.py:452
  103.2 1.3 %copy.12 = f32[8,4]{0,1:T(4,128)} copy(f32[8,4]{1,0:T(8,128)} %get-tuple-element.11) | data formatting | bytes 256 | tf_op jit(solution)/shard_map/pallas_call | solution.py:452
  104.5 1.6 %copy.16 = bf16[1,1,640,128]{3,2,1,0:T(8,128)(2,1)} copy(bf16[1,1,640,128]{3,2,1,0:T(8,128)(2,1)} %bitcast.12) | data formatting | bytes 327680
  106.1 1.6 %copy.17 = bf16[1,1,640,128]{3,2,1,0:T(8,128)(2,1)} copy(bf16[1,1,640,128]{3,2,1,0:T(8,128)(2,1)} %bitcast.11) | data formatting | bytes 327680
  107.7 2.8 %copy.18 = bf16[1,1,128,7168]{3,2,1,0:T(8,128)(2,1)} copy(bf16[1,1,128,7168]{3,2,1,0:T(8,128)(2,1)} %bitcast.10) | data formatting | bytes 3670016

commit v2 on v1

v2 whole, which is shorter than its diff:
```python
import functools

import jax
import jax.numpy as jnp
from jax import lax
from jax.experimental import pallas as pl
from jax.experimental.pallas import tpu as pltpu
from jax.sharding import PartitionSpec as P

MESH = pl.DeviceIdType.MESH
F32 = jnp.float32
BF16 = jnp.bfloat16
SIDE = 4
CAP = 5
TOK = 8
ROWS = 16
NT = (((1,), (1,)), ((), ()))


def kernel(
    sections,
    grad_ref,
    routes_ref,
    probs_ref,
    weight_hbm,
    gate_hbm,
    up_hbm,
    slot_out,
    down_buf,
    prob_out,
    rows_buf,
    own_buf,
    weight_buf,
    pre_buf,
    pre_t,
    meta1,
    meta2,
    select,
    hid,
    gate_f,
    up_f,
    scaled,
    total,
    slot_total,
    part_send,
    part_recv,
    part2,
    z_recv,
    s1_recv,
    s2_recv,
    s3_recv,
    s4_recv,
    sib_recv,
    z_send,
    s1_send,
    s2_send,
    s3_send,
    s4_send,
    sib_send,
    meta_send,
    meta_recv,
    part_ssem,
    part_rsem,
    load_sem,
):
    half = rows_buf.shape[-1]
    mid = half // 2
    quarter = mid // 2
    s = lax.axis_index("pipe")
    node = lax.axis_index("node")
    local = lax.axis_index("local")
    h, k = node // 2, lax.rem(node, 2)
    x, y = local // SIDE, lax.rem(local, SIDE)

    def ring(value):
        return lax.rem(value + 2 * SIDE, SIDE)

    def at(section, plane, core, px, py):
        return {"pipe": section, "node": plane * 2 + core, "local": px * SIDE + py}

    def remote(src, dst, ssem, rsem, device):
        return pltpu.make_async_remote_copy(
            src_ref=src, dst_ref=dst, send_sem=ssem, recv_sem=rsem, device_id=device, device_id_type=MESH
        )

    def send(ref, ssem, rsem, device):
        remote(ref, ref, ssem, rsem, device).start()

    def drain(ref, sem):
        pltpu.make_async_copy(ref, ref, sem).wait()

    s_up = lax.rem(s + 1, sections)
    s_down = lax.rem(s + sections - 1, sections)
    h_first = ring(h + jnp.where(s == sections - 1, 1, 0))
    h_back = ring(h - jnp.where(s == 0, 1, 0))

    line = y * 2 + k
    grid = h * SIDE + x

    def line_peer(j):
        other = lax.rem(line + j, 2 * SIDE)
        return at(s, h, lax.rem(other, 2), x, other // 2)

    def grid_peer(j):
        other = lax.rem(grid + j, SIDE * SIDE)
        return at(s, other // SIDE, k, lax.rem(other, SIDE), y)

    loads = [
        pltpu.make_async_copy(gate_hbm, pre_buf.at[0], load_sem.at[0]),
        pltpu.make_async_copy(up_hbm, pre_buf.at[1], load_sem.at[1]),
        pltpu.make_async_copy(weight_hbm.at[:, 0:half], weight_buf.at[0:128], load_sem.at[2]),
        pltpu.make_async_copy(weight_hbm.at[:, half : 2 * half], weight_buf.at[128:256], load_sem.at[3]),
    ]
    for load in loads:
        load.start()

    barrier = pltpu.get_barrier_semaphore()

    def greet(device):
        pl.semaphore_signal(barrier, inc=1, device_id=device, device_id_type=MESH)

    greet(at(s_up, h_first, k, x, y))
    greet(at(s_up, ring(h_first - 1), k, x, y))

    @pl.loop(1, 2 * SIDE)
    def _(j):
        greet(line_peer(j))

    @pl.loop(1, SIDE * SIDE)
    def _(j):
        greet(grid_peer(j))

    own_buf[0:TOK, :] = grad_ref[:, 0:half]
    own_buf[TOK:ROWS, :] = grad_ref[:, half : 2 * half]

    base = y * 32 + k * ROWS
    lane = lax.broadcasted_iota(jnp.int32, (TOK, 128), 1)
    token = lax.broadcasted_iota(jnp.int32, (TOK, 128), 0)
    place_own = jnp.where(lane - base == token, 1.0, 0.0).astype(BF16)
    own_routes = jnp.dot(routes_ref[...].astype(F32).astype(BF16), place_own, preferred_element_type=F32)
    own_probs = jnp.dot(probs_ref[...], place_own, preferred_element_type=F32)
    picks = own_routes.shape[0]
    row16 = lax.broadcasted_iota(jnp.int32, (ROWS, 128), 0).astype(F32)
    tile = jnp.zeros((ROWS, 128), F32)
    for pick in range(picks):
        tile = tile + jnp.where(own_routes[pick : pick + 1] == row16, own_probs[pick : pick + 1], 0.0)
    meta1[line] = tile.astype(BF16)

    pl.semaphore_wait(barrier, 2 + (2 * SIDE - 1) + (SIDE * SIDE - 1))

    def z_copy(src, wave, hsrc, section, plane):
        return remote(
            src, rows_buf.at[hsrc, x, y, k], z_send.at[wave], z_recv.at[wave], at(section, plane, k, x, y)
        )

    z_copy(own_buf, 0, h, s_down, h_back).start()
    z_copy(own_buf, 1, h, s_down, ring(h_back + 1)).start()

    @pl.loop(1, 2 * SIDE)
    def _(j):
        send(meta1.at[line], meta_send.at[0], meta_recv.at[0], line_peer(j))

    swap = jnp.where(s == sections - 1, 1, 0)

    def offset(wave):
        return jnp.where(wave == 2, 2 + swap, jnp.where(wave == 3, 3 - swap, wave))

    def source(wave):
        return lax.rem(h_first + SIDE - offset(wave), SIDE)

    def z_wait(wave):
        hw = source(wave)
        drain(rows_buf.at[hw, x, y, k], z_recv.at[offset(wave)])

    left, right = (0, mid), (mid, mid)

    def part(cols, piece):
        return pl.ds(cols[0] + piece * quarter, quarter)

    def blk(hw, px, py, cols):
        return rows_buf.at[hw, px, py, k, :, cols]

    halves = (pl.ds(*left), pl.ds(*right))
    lcols, rcols = halves
    full = pl.ds(0, half)
    x_up, x_down, x_far = ring(x + 1), ring(x - 1), ring(x + 2)
    y_up, y_down, y_far = ring(y + 1), ring(y - 1), ring(y + 2)
    dev_x = (at(s, h, k, x_up, y), at(s, h, k, x_down, y))
    dev_y = (at(s, h, k, x, y_up), at(s, h, k, x, y_down))
    sibling = at(s, h, 1 - k, x, y)
    from_x, from_y = (x_down, x_up, x_far), (y_down, y_up, y_far)

    def hand(ref, w):
        send(ref, sib_send.at[w], sib_recv.at[w], sibling)

    def step1(w):
        mine = blk(source(w), x, y, full)
        for d in range(2):
            send(mine, s1_send.at[w], s1_recv.at[w, d], dev_x[d])
            send(mine, s1_send.at[w], s1_recv.at[w, 2 + d], dev_y[d])
        hand(mine, w)

    def step2(w):
        hw = source(w)
        for d in range(2):
            drain(blk(hw, from_x[d], y, full), s1_recv.at[w, d])
            send(blk(hw, from_x[d], y, halves[d]), s2_send.at[w], s2_recv.at[w, 0], dev_x[d])
            for e in range(2):
                send(blk(hw, from_x[d], y, lcols), s3_send.at[w], s3_recv.at[w, e, d], dev_y[e])
            drain(blk(hw, x, from_y[d], full), s1_recv.at[w, 2 + d])
            send(blk(hw, x, from_y[d], halves[d]), s2_send.at[w], s2_recv.at[w, 1], dev_y[d])
            for e in range(2):
                send(blk(hw, x, from_y[d], rcols), s3_send.at[w], s3_recv.at[w, 2 + e, d], dev_x[e])
        for d in range(2):
            hand(blk(hw, from_x[d], y, full), w)
            hand(blk(hw, x, from_y[d], full), w)

    def step3(w):
        hw = source(w)
        drain(blk(hw, x_far, y, full), s2_recv.at[w, 0])
        for e in range(2):
            send(blk(hw, x_far, y, lcols), s3_send.at[w], s3_recv.at[w, e, 2], dev_y[e])
        drain(blk(hw, x, y_far, full), s2_recv.at[w, 1])
        for e in range(2):
            send(blk(hw, x, y_far, rcols), s3_send.at[w], s3_recv.at[w, 2 + e, 2], dev_x[e])
        hand(blk(hw, x_far, y, full), w)
        hand(blk(hw, x, y_far, full), w)

    def step4(w):
        hw = source(w)
        for j in range(3):
            for e in range(2):
                drain(blk(hw, from_x[j], from_y[e], lcols), s3_recv.at[w, e, j])
                send(blk(hw, from_x[j], from_y[e], part(left, e)), s4_send.at[w], s4_recv.at[w, 0], dev_y[e])
                drain(blk(hw, from_x[e], from_y[j], rcols), s3_recv.at[w, 2 + e, j])
                send(blk(hw, from_x[e], from_y[j], part(right, e)), s4_send.at[w], s4_recv.at[w, 1], dev_x[e])
        for j in range(3):
            for e in range(2):
                hand(blk(hw, from_x[j], from_y[e], lcols), w)
                hand(blk(hw, from_x[e], from_y[j], rcols), w)

    def step5(w):
        hw = source(w)
        drain(rows_buf.at[hw, 0:3, y_far, k, :, lcols], s4_recv.at[w, 0])
        for j in range(3):
            hand(blk(hw, from_x[j], y_far, lcols), w)
        drain(rows_buf.at[hw, x_far, 0:3, k, :, rcols], s4_recv.at[w, 1])
        for j in range(3):
            hand(blk(hw, x_far, from_y[j], rcols), w)

    def arrived(w):
        drain(rows_buf.at[source(w), :, :, 1 - k], sib_recv.at[w])

    def sent(w):
        drain(rows_buf.at[0, 0, :, 0], s1_send.at[w])
        drain(rows_buf.at[0, 0, 0:2, 0], s2_send.at[w])
        drain(rows_buf.at[0, 0:3, 0:2, 0], s3_send.at[w])
        drain(rows_buf.at[0, 0, 0:3, 0], s4_send.at[w])
        drain(rows_buf.at[0, :, :, 0], sib_send.at[w])

    z_wait(0)
    z_copy(rows_buf.at[h_first, x, y, k], 3, h_first, s, ring(h - 1)).start()
    step1(0)

    drain(meta1.at[0 : 2 * SIDE - 1], meta_recv.at[0])
    meta2[grid] = jnp.sum(meta1[...].astype(F32), axis=0).astype(BF16)

    @pl.loop(1, SIDE * SIDE)
    def _(j):
        send(meta2.at[grid], meta_send.at[1], meta_recv.at[1], grid_peer(j))

    step2(0)
    z_wait(1)
    z_copy(rows_buf.at[source(1), x, y, k], 2, source(1), s, ring(h + 1)).start()
    step1(1)

    step3(0)
    step2(1)
    drain(meta2.at[0 : SIDE * SIDE - 1], meta_recv.at[1])
    for load in loads:
        load.wait()
    pre_t[...] = jnp.concatenate([pre_buf[0], pre_buf[1]], axis=1).astype(F32).T.astype(BF16)
    tokens = SIDE * 128
    slots = slot_total.shape[0]

    def prepare(w):
        hw = source(w)
        tiles = jnp.concatenate([meta2[hw * SIDE + j] for j in range(SIDE)], axis=1).astype(F32)
        rows = lax.broadcasted_iota(jnp.int32, (ROWS, tokens), 0)
        prob = jnp.sum(jnp.where(rows == node, tiles, 0.0), axis=0, keepdims=True)
        prob8 = jnp.broadcast_to(prob, (8, tokens))
        hit = jnp.where(prob8 > 0.0, 1.0, 0.0)
        at_lane = lax.broadcasted_iota(jnp.int32, (8, tokens), 1)
        place = lax.rem(at_lane, ROWS)
        rank = jnp.zeros((8, tokens), F32)
        for back in range(1, TOK):
            rank = rank + jnp.where(place >= back, pltpu.roll(hit, back, axis=1), 0.0)
        group = (at_lane // 32) * (2 * SIDE) + 2 * hw + lax.rem(at_lane // ROWS, 2)
        slot = jnp.where(prob8 > 0.0, group * CAP + rank.astype(jnp.int32), -1)[0:1]
        slot_row = lax.broadcasted_iota(jnp.int32, (slots, tokens), 0)
        select[hw] = jnp.where(slot_row == slot, 1.0, 0.0).astype(BF16)
        moved = jnp.dot(pre_t[...], select[hw], preferred_element_type=F32)
        gate, up = moved[0:128], moved[128:256]
        sig = 1.0 / (1.0 + jnp.exp(-gate))
        act = gate * sig
        hidden = act * up
        hid[hw] = hidden
        gate_f[hw] = prob * (up * sig * (1.0 + gate * (1.0 - sig)))
        up_f[hw] = prob * act
        scaled_hidden = prob * hidden
        scaled[hw, 0:128] = scaled_hidden.astype(BF16)
        scaled[hw, 128:256] = pltpu.roll(scaled_hidden, TOK, axis=1).astype(BF16)

    def scores_of(w, j):
        hw = source(w)
        block = rows_buf[hw, pl.ds(2 * j, 2)].reshape(256, half)
        both = lax.dot_general(weight_buf[...], block, NT, preferred_element_type=F32)
        scores = both[0:128] + pltpu.roll(both[128:256], 256 - TOK, axis=1)
        cols = pl.ds(j * 256, 256)
        shares = jnp.sum((hid[hw, :, cols] * scores).reshape(ROWS, 8, 256), axis=0)
        part_send[hw, 2 * j] = shares[:, 0:128]
        part_send[hw, 2 * j + 1] = shares[:, 128:256]
        d_gate = (gate_f[hw, :, cols] * scores).astype(BF16)
        d_up = (up_f[hw, :, cols] * scores).astype(BF16)
        moved = lax.dot_general(
            select[hw, :, cols], jnp.concatenate([d_gate, d_up], axis=0), NT, preferred_element_type=F32
        )
        if j == 0:

            @pl.when(w == 0)
            def _():
                slot_total[...] = moved

            @pl.when(w > 0)
            def _():
                slot_total[...] += moved

        else:
            slot_total[...] += moved

    def share(w):
        hw = source(w)

        @pl.loop(0, SIDE)
        def _(px):
            own = (hw == h) & (px == x)

            @pl.when(own)
            def _():
                part_recv[grid] = part_send[hw, px]

            @pl.when(jnp.logical_not(own))
            def _():
                remote(
                    part_send.at[hw, px], part_recv.at[grid], part_ssem.at[0], part_rsem.at[0], at(s, hw, k, px, y)
                ).start()

    def down_of(w, low, high, last):
        hw = source(w)

        @pl.loop(low, high)
        def _(c):
            cols = pl.ds(pl.multiple_of(c * 512, 512), 512)
            block = rows_buf[hw, :, :, :, :, cols].reshape(tokens, 512)
            more = jnp.dot(scaled[hw], block, preferred_element_type=F32)
            if last:
                down_buf[:, cols] = (total[:, cols] + more).astype(BF16)
            else:

                @pl.when(w == 0)
                def _():
                    total[:, cols] = more

                @pl.when(w > 0)
                def _():
                    total[:, cols] += more

    tiles_of_down = half // 512
    prepare(0)
    step4(0)
    z_wait(2)
    step1(2)

    @pl.loop(1, SIDE)
    def _(w):
        step3(w)
        step5(w - 1)

        @pl.when(w < SIDE - 1)
        def _():
            step2(w + 1)

        prepare(w)
        arrived(w - 1)
        scores_of(w - 1, 0)
        step4(w)

        @pl.when(w < SIDE - 2)
        def _():
            z_wait(w + 2)
            step1(w + 2)

        scores_of(w - 1, 1)
        share(w - 1)
        down_of(w - 1, 0, tiles_of_down, False)

    step5(SIDE - 1)
    arrived(SIDE - 1)
    scores_of(SIDE - 1, 0)
    scores_of(SIDE - 1, 1)
    share(SIDE - 1)
    down_of(SIDE - 1, 0, tiles_of_down, True)
    slot_out[0] = slot_total[:, 0:128].astype(BF16)
    slot_out[1] = slot_total[:, 128:256].astype(BF16)

    drain(part_recv.at[0 : SIDE * SIDE - 1], part_rsem.at[0])
    row8 = lax.broadcasted_iota(jnp.int32, (8, 128), 0)
    tile = jnp.zeros((8, 128), F32)
    for plane in range(SIDE):
        over_x = part_recv[plane * SIDE]
        for px in range(1, SIDE):
            over_x = over_x + part_recv[plane * SIDE + px]
        tile = tile + jnp.where(row8 == plane, jnp.sum(over_x, axis=0, keepdims=True), 0.0)
    part2[line] = tile

    @pl.loop(1, 2 * SIDE)
    def _(j):
        send(part2.at[line], part_ssem.at[1], part_rsem.at[1], line_peer(j))

    @pl.loop(0, SIDE)
    def _(w):
        sent(w)
        drain(rows_buf.at[0, 0, 0, 0], z_send.at[w])

    drain(meta1.at[0 : 2 * SIDE - 1], meta_send.at[0])
    drain(meta2.at[0 : SIDE * SIDE - 1], meta_send.at[1])
    drain(part_recv.at[0 : SIDE * SIDE - 1], part_ssem.at[0])

    drain(part2.at[0 : 2 * SIDE - 1], part_rsem.at[1])
    result = jnp.zeros((8, 128), F32)
    row8f = row8.astype(F32)
    for pick in range(picks):
        for core in range(2):
            over_y = part2[core]
            for py in range(1, SIDE):
                over_y = over_y + part2[py * 2 + core]
            chosen = jnp.where(own_routes[pick : pick + 1] == row8f * 2.0 + core, over_y, 0.0)
            result = result + jnp.where(row8 == pick, jnp.sum(chosen, axis=0, keepdims=True), 0.0)
    prob_out[...] = pltpu.roll(result, lax.rem(128 - base, 128), axis=1)[0:picks, 0:TOK]
    drain(part2.at[0 : 2 * SIDE - 1], part_ssem.at[1])


def publish(slot_in, down_in, prob_in, gate_out, up_out, down_out, prob_out, sem):
    half = down_in.shape[1]
    hidden = down_in.shape[0] // 2
    moves = [
        pltpu.make_async_copy(down_in.at[0:hidden], down_out.at[:, 0:half], sem.at[0]),
        pltpu.make_async_copy(down_in.at[hidden : 2 * hidden], down_out.at[:, half : 2 * half], sem.at[1]),
        pltpu.make_async_copy(slot_in.at[0], gate_out, sem.at[2]),
        pltpu.make_async_copy(slot_in.at[1], up_out, sem.at[3]),
        pltpu.make_async_copy(prob_in, prob_out, sem.at[4]),
    ]
    for move in moves:
        move.start()
    for move in moves:
        move.wait()


def shards(next_grad, routes, probs, down_weight, gate_pre, up_pre):
    sections = lax.axis_size("pipe")
    grad = next_grad[0]
    weight = down_weight[0, 0]
    gate_rows = gate_pre[0, 0]
    slots, hidden = gate_rows.shape
    width = grad.shape[1]
    picks = routes.shape[2]
    half = width // 2
    tokens = SIDE * 128
    vmem = pl.BlockSpec(memory_space=pltpu.VMEM)
    hbm = pl.BlockSpec(memory_space=pl.ANY)
    dma = pltpu.SemaphoreType.DMA
    slot_grads, down_halves, prob_t = pl.pallas_call(
        functools.partial(kernel, sections),
        out_shape=(
            pltpu.VMEM((2, slots, hidden), BF16),
            pltpu.VMEM((2 * hidden, half), BF16),
            pltpu.VMEM((picks, TOK), F32),
        ),
        in_specs=[vmem, vmem, vmem, hbm, hbm, hbm],
        out_specs=(vmem, vmem, vmem),
        scratch_shapes=[
            pltpu.VMEM((SIDE, SIDE, SIDE, 2, ROWS, half), BF16),
            pltpu.VMEM((ROWS, half), BF16),
            pltpu.VMEM((2 * hidden, half), BF16),
            pltpu.VMEM((2, slots, hidden), BF16),
            pltpu.VMEM((2 * hidden, slots), BF16),
            pltpu.VMEM((2 * SIDE, ROWS, 128), BF16),
            pltpu.VMEM((SIDE * SIDE, ROWS, 128), BF16),
            pltpu.VMEM((SIDE, slots, tokens), BF16),
            pltpu.VMEM((SIDE, hidden, tokens), F32),
            pltpu.VMEM((SIDE, hidden, tokens), F32),
            pltpu.VMEM((SIDE, hidden, tokens), F32),
            pltpu.VMEM((SIDE, 2 * hidden, tokens), BF16),
            pltpu.VMEM((2 * hidden, half), F32),
            pltpu.VMEM((slots, 2 * hidden), F32),
            pltpu.VMEM((SIDE, SIDE, 8, 128), F32),
            pltpu.VMEM((SIDE * SIDE, 8, 128), F32),
            pltpu.VMEM((2 * SIDE, 8, 128), F32),
            dma((SIDE,)),
            dma((SIDE, 4)),
            dma((SIDE, 2)),
            dma((SIDE, 4, 3)),
            dma((SIDE, 2)),
            dma((SIDE,)),
            dma((SIDE,)),
            dma((SIDE,)),
            dma((SIDE,)),
            dma((SIDE,)),
            dma((SIDE,)),
            dma((SIDE,)),
            dma((2,)),
            dma((2,)),
            dma((2,)),
            dma((2,)),
            dma((4,)),
        ],
        compiler_params=pltpu.CompilerParams(
            collective_id=0, has_side_effects=True, vmem_limit_bytes=52 * 1024 * 1024
        ),
        cost_estimate=pl.CostEstimate(
            flops=4 * slots * hidden * width, bytes_accessed=4 * hidden * width, transcendentals=slots * hidden
        ),
    )(grad, routes[0].T, probs[0].T, weight, gate_rows, up_pre[0, 0])
    gate_grad, up_grad, down_grad, prob_grad = pl.pallas_call(
        publish,
        out_shape=(
            jax.ShapeDtypeStruct((slots, hidden), BF16),
            jax.ShapeDtypeStruct((slots, hidden), BF16),
            jax.ShapeDtypeStruct((hidden, width), BF16),
            jax.ShapeDtypeStruct((picks, TOK), F32),
        ),
        in_specs=[vmem, vmem, vmem],
        out_specs=(hbm, hbm, hbm, hbm),
        scratch_shapes=[dma((5,))],
    )(slot_grads, down_halves, prob_t)
    return (gate_grad[None, None], up_grad[None, None], down_grad[None, None], prob_grad.T[None])


def solution(mesh):
    return jax.shard_map(
        shards,
        mesh=mesh,
        in_specs=(
            P("pipe", ("node", "local"), None),
            P("pipe", ("node", "local"), None),
            P("pipe", ("node", "local"), None),
            P("pipe", "node", "local", None),
            P("pipe", "node", None, "local"),
            P("pipe", "node", None, "local"),
        ),
        out_specs=(
            P("pipe", "node", None, "local"),
            P("pipe", "node", None, "local"),
            P("pipe", "node", "local", None),
            P("pipe", ("node", "local"), None),
        ),
        check_vma=False,
    )
```

time: 111 us -> 91.1 us (0.82)
  the two profiles are of different devices: /device:TPU:64 before, /device:TPU:97 now
where the time goes in v2:
time: 91.1 us; the launch traced here: 90.9 us
  Pallas kernels  87.7 us (96%)
  local copies, waits for them, and re-layouts  2.56 us (3%)
    pallas_call x1, Pallas kernels, shards(): pl.pallas_call(functools.partial(kernel, sections), out_shape=(pltpu.VMEM...  84.8 us
    pallas_call x1, Pallas kernels, shards(): pl.pallas_call(publish, out_shape=(jax.ShapeDtypeStruct((slots, hidden),...  2.89 us
    unnamed x6, local copies, waits for them, and re-layouts  2.56 us

profile of v2, /device:TPU:97, one launch (start us, length us, event | category | flops | bytes accessed | tf_op | source)
XLA Modules:
  0.0 90.9 jit_solution(15640729718246085789)
XLA Ops:
  0.6 84.8 %shard_map.93 = (bf16[2,640,128]{2,1,0:T(8,128)(2,1)S(1)}, bf16[256,3584]{1,0:T(8,128)(2,1)S(1)}, f32[4,8]{1,0:T(4,128)S(1)}) custom-call(bf16[8,7168]{1,0:T(8,128)(2,1)} %bitcast.22, s32[4,8]{1,0:T(4,128)} %bitcast.23, bf16[4,8]{1,0:T(4,128)(2,1)} %bitcast.25, bf16[128,7168]{1,0:T(8,128)(2,1)} %bitcast.16, bf16[640,128]{1,0:T(8,128)(2,1)} %bitcast.18, ...), custom_call_target="tpu_custom_call" | custom-call | flops 2348810240 | bytes 3670016 | tf_op jit(solution)/shard_map/pallas_call | solution.py:482
  85.5 0.0 copy-start
  85.5 1.2 %copy-done = bf16[256,3584]{1,0:T(8,128)(2,1)} copy-done((bf16[256,3584]{1,0:T(8,128)(2,1)}, bf16[256,3584]{1,0:T(8,128)(2,1)S(1)}, u32[]{:S(2)}) %copy-start) | copy-done | bytes 1835032
  86.7 0.0 copy-start.1
  86.7 0.7 copy-done.1
  87.5 0.0 copy-start.2
  87.5 0.6 copy-done.2
  88.0 2.9 %shard_map.94 = (bf16[640,128]{1,0:T(8,128)(2,1)}, bf16[640,128]{1,0:T(8,128)(2,1)}, bf16[128,7168]{1,0:T(8,128)(2,1)}, f32[4,8]{1,0:T(4,128)}) custom-call(bf16[2,640,128]{2,1,0:T(8,128)(2,1)} %copy-done.1, bf16[256,3584]{1,0:T(8,128)(2,1)} %copy-done, f32[4,8]{1,0:T(4,128)} %copy-done.2), custom_call_target="tpu_custom_call" | custom-call | tf_op jit(solution)/shard_map/pallas_call | solution.py:534
Async XLA Ops:
  85.5 1.3 %copy-start = (bf16[256,3584]{1,0:T(8,128)(2,1)}, bf16[256,3584]{1,0:T(8,128)(2,1)S(1)}, u32[]{:S(2)}) copy-start(bf16[256,3584]{1,0:T(8,128)(2,1)S(1)} %get-tuple-element.12.down_in) | copy-start | bytes 5505028
  86.7 0.7 copy-start.1
  87.5 0.6 copy-start.2

commit v3 on v2

--- a/solution.py
+++ b/solution.py
@@ -44,7 +44,6 @@
     slot_total,
     part_send,
     part_recv,
-    part2,
     z_recv,
     s1_recv,
     s2_recv,
@@ -95,6 +94,7 @@
     h_back = ring(h - jnp.where(s == 0, 1, 0))
 
     line = y * 2 + k
+    me = node * SIDE * SIDE + local
     grid = h * SIDE + x
 
     def line_peer(j):
@@ -317,7 +317,7 @@
         both = lax.dot_general(weight_buf[...], block, NT, preferred_element_type=F32)
         scores = both[0:128] + pltpu.roll(both[128:256], 256 - TOK, axis=1)
         cols = pl.ds(j * 256, 256)
-        shares = jnp.sum((hid[hw, :, cols] * scores).reshape(ROWS, 8, 256), axis=0)
+        shares = jnp.sum(hid[hw, :, cols] * scores, axis=0, keepdims=True)
         part_send[hw, 2 * j] = shares[:, 0:128]
         part_send[hw, 2 * j + 1] = shares[:, 128:256]
         d_gate = (gate_f[hw, :, cols] * scores).astype(BF16)
@@ -341,18 +341,19 @@
     def share(w):
         hw = source(w)
 
-        @pl.loop(0, SIDE)
-        def _(px):
-            own = (hw == h) & (px == x)
+        @pl.loop(0, 8 * SIDE)
+        def _(j):
+            px, py, core = j // 8, lax.rem(j // 2, SIDE), lax.rem(j, 2)
+            own = (hw == h) & (px == x) & (py == y) & (core == k)
 
             @pl.when(own)
             def _():
-                part_recv[grid] = part_send[hw, px]
+                part_recv[me] = part_send[hw, px]
 
             @pl.when(jnp.logical_not(own))
             def _():
                 remote(
-                    part_send.at[hw, px], part_recv.at[grid], part_ssem.at[0], part_rsem.at[0], at(s, hw, k, px, y)
+                    part_send.at[hw, px], part_recv.at[me], part_ssem.at[0], part_rsem.at[0], at(s, hw, core, px, py)
                 ).start()
 
     def down_of(w, low, high, last):
@@ -413,20 +414,6 @@
     slot_out[0] = slot_total[:, 0:128].astype(BF16)
     slot_out[1] = slot_total[:, 128:256].astype(BF16)
 
-    drain(part_recv.at[0 : SIDE * SIDE - 1], part_rsem.at[0])
-    row8 = lax.broadcasted_iota(jnp.int32, (8, 128), 0)
-    tile = jnp.zeros((8, 128), F32)
-    for plane in range(SIDE):
-        over_x = part_recv[plane * SIDE]
-        for px in range(1, SIDE):
-            over_x = over_x + part_recv[plane * SIDE + px]
-        tile = tile + jnp.where(row8 == plane, jnp.sum(over_x, axis=0, keepdims=True), 0.0)
-    part2[line] = tile
-
-    @pl.loop(1, 2 * SIDE)
-    def _(j):
-        send(part2.at[line], part_ssem.at[1], part_rsem.at[1], line_peer(j))
-
     @pl.loop(0, SIDE)
     def _(w):
         sent(w)
@@ -434,20 +421,20 @@
 
     drain(meta1.at[0 : 2 * SIDE - 1], meta_send.at[0])
     drain(meta2.at[0 : SIDE * SIDE - 1], meta_send.at[1])
-    drain(part_recv.at[0 : SIDE * SIDE - 1], part_ssem.at[0])
-
-    drain(part2.at[0 : 2 * SIDE - 1], part_rsem.at[1])
+
+    others = part_recv.at[0 : part_recv.shape[0] - 1]
+    drain(others, part_ssem.at[0])
+    drain(others, part_rsem.at[0])
+    row8 = lax.broadcasted_iota(jnp.int32, (8, 128), 0)
     result = jnp.zeros((8, 128), F32)
-    row8f = row8.astype(F32)
-    for pick in range(picks):
-        for core in range(2):
-            over_y = part2[core]
-            for py in range(1, SIDE):
-                over_y = over_y + part2[py * 2 + core]
-            chosen = jnp.where(own_routes[pick : pick + 1] == row8f * 2.0 + core, over_y, 0.0)
-            result = result + jnp.where(row8 == pick, jnp.sum(chosen, axis=0, keepdims=True), 0.0)
+    for m in range(2 * SIDE):
+        share_sum = part_recv[m * SIDE * SIDE]
+        for j in range(1, SIDE * SIDE):
+            share_sum = share_sum + part_recv[m * SIDE * SIDE + j]
+        for pick in range(picks):
+            chosen = jnp.where(own_routes[pick : pick + 1] == m, share_sum, 0.0)
+            result = result + jnp.where(row8 == pick, chosen, 0.0)
     prob_out[...] = pltpu.roll(result, lax.rem(128 - base, 128), axis=1)[0:picks, 0:TOK]
-    drain(part2.at[0 : 2 * SIDE - 1], part_ssem.at[1])
 
 
 def publish(slot_in, down_in, prob_in, gate_out, up_out, down_out, prob_out, sem):
@@ -503,9 +490,8 @@
             pltpu.VMEM((SIDE, 2 * hidden, tokens), BF16),
             pltpu.VMEM((2 * hidden, half), F32),
             pltpu.VMEM((slots, 2 * hidden), F32),
-            pltpu.VMEM((SIDE, SIDE, 8, 128), F32),
-            pltpu.VMEM((SIDE * SIDE, 8, 128), F32),
-            pltpu.VMEM((2 * SIDE, 8, 128), F32),
+            pltpu.VMEM((SIDE, SIDE, 1, 128), F32),
+            pltpu.VMEM((2 * SIDE * SIDE * SIDE, 1, 128), F32),
             dma((SIDE,)),
             dma((SIDE, 4)),
             dma((SIDE, 2)),
@@ -520,8 +506,8 @@
             dma((SIDE,)),
             dma((2,)),
             dma((2,)),
-            dma((2,)),
-            dma((2,)),
+            dma((1,)),
+            dma((1,)),
             dma((4,)),
         ],
         compiler_params=pltpu.CompilerParams(
@@ -542,6 +528,7 @@
         in_specs=[vmem, vmem, vmem],
         out_specs=(hbm, hbm, hbm, hbm),
         scratch_shapes=[dma((5,))],
+        compiler_params=pltpu.CompilerParams(vmem_limit_bytes=1024 * 1024),
     )(slot_grads, down_halves, prob_t)
     return (gate_grad[None, None], up_grad[None, None], down_grad[None, None], prob_grad.T[None])
 

time: 91.1 us -> 86.2 us (0.946)
  the two profiles are of different devices: /device:TPU:97 before, /device:TPU:64 now
where the time goes in v3:
time: 86.2 us; the launch traced here: 86.1 us
  Pallas kernels  85.4 us (99%)
    pallas_call x1, Pallas kernels, shards(): pl.pallas_call(functools.partial(kernel, sections), out_shape=(pltpu.VMEM...  84.1 us

profile of v3, /device:TPU:64, one launch (start us, length us, event | category | flops | bytes accessed | tf_op | source)
XLA Modules:
  0.0 86.1 jit_solution(14092460142194834346)
XLA Ops:
  0.6 84.1 %shard_map.93 = (bf16[2,640,128]{2,1,0:T(8,128)(2,1)S(1)}, bf16[256,3584]{1,0:T(8,128)(2,1)S(1)}, f32[4,8]{1,0:T(4,128)S(1)}) custom-call(bf16[8,7168]{1,0:T(8,128)(2,1)} %bitcast.22, s32[4,8]{1,0:T(4,128)} %bitcast.23, bf16[4,8]{1,0:T(4,128)(2,1)} %bitcast.25, bf16[128,7168]{1,0:T(8,128)(2,1)} %bitcast.16, bf16[640,128]{1,0:T(8,128)(2,1)} %bitcast.18, ...), custom_call_target="tpu_custom_call" | custom-call | flops 2348810240 | bytes 3670016 | tf_op jit(solution)/shard_map/pallas_call | solution.py:469
  84.7 1.4 %shard_map.94 = (bf16[640,128]{1,0:T(8,128)(2,1)}, bf16[640,128]{1,0:T(8,128)(2,1)}, bf16[128,7168]{1,0:T(8,128)(2,1)}, f32[4,8]{1,0:T(4,128)}) custom-call(bf16[2,640,128]{2,1,0:T(8,128)(2,1)S(1)} %get-tuple-element.11.slot_in, bf16[256,3584]{1,0:T(8,128)(2,1)S(1)} %get-tuple-element.12.down_in, f32[4,8]{1,0:T(4,128)S(1)} %get-tuple-element.13.prob_in), custom_call_target="tpu_custom_call" | custom-call | tf_op jit(solution)/shard_map/pallas_call | solution.py:520

commit v4 on v3

--- a/solution.py
+++ b/solution.py
@@ -30,6 +30,7 @@
     prob_out,
     rows_buf,
     own_buf,
+    far_buf,
     weight_buf,
     pre_buf,
     pre_t,
@@ -42,6 +43,7 @@
     scaled,
     total,
     slot_total,
+    score_buf,
     part_send,
     part_recv,
     z_recv,
@@ -61,6 +63,9 @@
     part_ssem,
     part_rsem,
     load_sem,
+    far_sem,
+    far_send,
+    far_recv,
 ):
     half = rows_buf.shape[-1]
     mid = half // 2
@@ -101,9 +106,51 @@
         other = lax.rem(line + j, 2 * SIDE)
         return at(s, h, lax.rem(other, 2), x, other // 2)
 
-    def grid_peer(j):
-        other = lax.rem(grid + j, SIDE * SIDE)
-        return at(s, other // SIDE, k, lax.rem(other, SIDE), y)
+    def plane_peer(j):
+        return at(s, h, k, ring(x + j), y)
+
+    planes = (at(s, ring(h + 1), k, x, y), at(s, ring(h - 1), k, x, y))
+
+    barrier = pltpu.get_barrier_semaphore()
+
+    def greet(device):
+        pl.semaphore_signal(barrier, inc=1, device_id=device, device_id_type=MESH)
+
+    greet(at(s_up, h_first, k, x, y))
+    greet(at(s_up, ring(h_first - 1), k, x, y))
+
+    @pl.loop(1, 2 * SIDE)
+    def _(j):
+        greet(line_peer(j))
+
+    for j in range(1, SIDE):
+        greet(plane_peer(j))
+    for device in planes:
+        greet(device)
+    diagonal = at(s, h, k, ring(x + 2), ring(y + 2))
+    greet(diagonal)
+
+    own_buf[0:TOK, :] = grad_ref[:, 0:half]
+    own_buf[TOK:ROWS, :] = grad_ref[:, half : 2 * half]
+
+    pl.semaphore_wait(barrier, 2 + (2 * SIDE - 1) + (SIDE - 1) + 2 + 1)
+
+    def z_copy(src, wave, hsrc, section, plane):
+        return remote(
+            src, rows_buf.at[hsrc, x, y, k], z_send.at[wave], z_recv.at[wave], at(section, plane, k, x, y)
+        )
+
+    halves = (pl.ds(0, mid), pl.ds(mid, mid))
+    for i in range(2):
+        remote(
+            own_buf.at[:, halves[i]],
+            rows_buf.at[h, x, y, k, :, halves[i]],
+            z_send.at[0],
+            z_recv.at[SIDE * i],
+            at(s_down, h_back, k, x, y),
+        ).start()
+    z_copy(own_buf, 1, h, s_down, ring(h_back + 1)).start()
+    remote(own_buf, far_buf, far_sem.at[0], far_sem.at[1], diagonal).start()
 
     loads = [
         pltpu.make_async_copy(gate_hbm, pre_buf.at[0], load_sem.at[0]),
@@ -113,25 +160,6 @@
     ]
     for load in loads:
         load.start()
-
-    barrier = pltpu.get_barrier_semaphore()
-
-    def greet(device):
-        pl.semaphore_signal(barrier, inc=1, device_id=device, device_id_type=MESH)
-
-    greet(at(s_up, h_first, k, x, y))
-    greet(at(s_up, ring(h_first - 1), k, x, y))
-
-    @pl.loop(1, 2 * SIDE)
-    def _(j):
-        greet(line_peer(j))
-
-    @pl.loop(1, SIDE * SIDE)
-    def _(j):
-        greet(grid_peer(j))
-
-    own_buf[0:TOK, :] = grad_ref[:, 0:half]
-    own_buf[TOK:ROWS, :] = grad_ref[:, half : 2 * half]
 
     base = y * 32 + k * ROWS
     lane = lax.broadcasted_iota(jnp.int32, (TOK, 128), 1)
@@ -146,16 +174,6 @@
         tile = tile + jnp.where(own_routes[pick : pick + 1] == row16, own_probs[pick : pick + 1], 0.0)
     meta1[line] = tile.astype(BF16)
 
-    pl.semaphore_wait(barrier, 2 + (2 * SIDE - 1) + (SIDE * SIDE - 1))
-
-    def z_copy(src, wave, hsrc, section, plane):
-        return remote(
-            src, rows_buf.at[hsrc, x, y, k], z_send.at[wave], z_recv.at[wave], at(section, plane, k, x, y)
-        )
-
-    z_copy(own_buf, 0, h, s_down, h_back).start()
-    z_copy(own_buf, 1, h, s_down, ring(h_back + 1)).start()
-
     @pl.loop(1, 2 * SIDE)
     def _(j):
         send(meta1.at[line], meta_send.at[0], meta_recv.at[0], line_peer(j))
@@ -180,7 +198,6 @@
     def blk(hw, px, py, cols):
         return rows_buf.at[hw, px, py, k, :, cols]
 
-    halves = (pl.ds(*left), pl.ds(*right))
     lcols, rcols = halves
     full = pl.ds(0, half)
     x_up, x_down, x_far = ring(x + 1), ring(x - 1), ring(x + 2)
@@ -193,12 +210,11 @@
     def hand(ref, w):
         send(ref, sib_send.at[w], sib_recv.at[w], sibling)
 
-    def step1(w):
-        mine = blk(source(w), x, y, full)
+    def step1(w, cols):
+        mine = blk(source(w), x, y, cols)
         for d in range(2):
             send(mine, s1_send.at[w], s1_recv.at[w, d], dev_x[d])
             send(mine, s1_send.at[w], s1_recv.at[w, 2 + d], dev_y[d])
-        hand(mine, w)
 
     def step2(w):
         hw = source(w)
@@ -228,25 +244,44 @@
 
     def step4(w):
         hw = source(w)
-        for j in range(3):
+        for j in range(2):
             for e in range(2):
                 drain(blk(hw, from_x[j], from_y[e], lcols), s3_recv.at[w, e, j])
                 send(blk(hw, from_x[j], from_y[e], part(left, e)), s4_send.at[w], s4_recv.at[w, 0], dev_y[e])
                 drain(blk(hw, from_x[e], from_y[j], rcols), s3_recv.at[w, 2 + e, j])
                 send(blk(hw, from_x[e], from_y[j], part(right, e)), s4_send.at[w], s4_recv.at[w, 1], dev_x[e])
-        for j in range(3):
+        hand(blk(hw, x, y, full), w)
+        for j in range(2):
             for e in range(2):
                 hand(blk(hw, from_x[j], from_y[e], lcols), w)
                 hand(blk(hw, from_x[e], from_y[j], rcols), w)
 
     def step5(w):
         hw = source(w)
-        drain(rows_buf.at[hw, 0:3, y_far, k, :, lcols], s4_recv.at[w, 0])
-        for j in range(3):
+        for e in range(2):
+            drain(blk(hw, x_far, from_y[e], lcols), s3_recv.at[w, e, 2])
+            hand(blk(hw, x_far, from_y[e], lcols), w)
+            drain(blk(hw, from_x[e], y_far, rcols), s3_recv.at[w, 2 + e, 2])
+            hand(blk(hw, from_x[e], y_far, rcols), w)
+        drain(rows_buf.at[hw, 0:2, y_far, k, :, lcols], s4_recv.at[w, 0])
+        drain(rows_buf.at[hw, x_far, 0:2, k, :, rcols], s4_recv.at[w, 1])
+        for j in range(2):
             hand(blk(hw, from_x[j], y_far, lcols), w)
-        drain(rows_buf.at[hw, x_far, 0:3, k, :, rcols], s4_recv.at[w, 1])
-        for j in range(3):
             hand(blk(hw, x_far, from_y[j], rcols), w)
+
+    def far_copy(src, index, hsrc, section, plane):
+        return remote(
+            src,
+            rows_buf.at[hsrc, x_far, y_far, k],
+            far_send.at[index],
+            far_recv.at[index],
+            at(section, plane, k, x, y),
+        )
+
+    def far_wait(w):
+        hw = source(w)
+        drain(rows_buf.at[hw, x_far, y_far, k], far_recv.at[offset(w)])
+        hand(rows_buf.at[hw, x_far, y_far, k], w)
 
     def arrived(w):
         drain(rows_buf.at[source(w), :, :, 1 - k], sib_recv.at[w])
@@ -255,28 +290,43 @@
         drain(rows_buf.at[0, 0, :, 0], s1_send.at[w])
         drain(rows_buf.at[0, 0, 0:2, 0], s2_send.at[w])
         drain(rows_buf.at[0, 0:3, 0:2, 0], s3_send.at[w])
-        drain(rows_buf.at[0, 0, 0:3, 0], s4_send.at[w])
+        drain(rows_buf.at[0, 0, 0:2, 0], s4_send.at[w])
         drain(rows_buf.at[0, :, :, 0], sib_send.at[w])
 
-    z_wait(0)
+    for i in range(2):
+        drain(rows_buf.at[h_first, x, y, k, :, halves[i]], z_recv.at[SIDE * i])
+        step1(0, halves[i])
     z_copy(rows_buf.at[h_first, x, y, k], 3, h_first, s, ring(h - 1)).start()
-    step1(0)
 
     drain(meta1.at[0 : 2 * SIDE - 1], meta_recv.at[0])
     meta2[grid] = jnp.sum(meta1[...].astype(F32), axis=0).astype(BF16)
 
-    @pl.loop(1, SIDE * SIDE)
-    def _(j):
-        send(meta2.at[grid], meta_send.at[1], meta_recv.at[1], grid_peer(j))
-
+    def pass_on(tile, kind):
+        for j in range(1, SIDE):
+            send(meta2.at[tile], meta_send.at[1], meta_recv.at[kind], plane_peer(j))
+
+    above, below, across = ring(h + 1) * SIDE + x, ring(h - 1) * SIDE + x, ring(h + 2) * SIDE + x
+    for device in planes:
+        send(meta2.at[grid], meta_send.at[1], meta_recv.at[1], device)
+    pass_on(grid, 2)
+    drain(far_buf, far_sem.at[1])
+    far_copy(far_buf, 0, h, s_down, h_back).start()
+    far_copy(far_buf, 1, h, s_down, ring(h_back + 1)).start()
     step2(0)
+    drain(meta2.at[0:2], meta_recv.at[1])
+    send(meta2.at[below], meta_send.at[1], meta_recv.at[3], planes[0])
+    pass_on(above, 4)
+    pass_on(below, 4)
     z_wait(1)
     z_copy(rows_buf.at[source(1), x, y, k], 2, source(1), s, ring(h + 1)).start()
-    step1(1)
+    step1(1, full)
 
     step3(0)
     step2(1)
-    drain(meta2.at[0 : SIDE * SIDE - 1], meta_recv.at[1])
+    drain(meta2.at[0], meta_recv.at[3])
+    pass_on(across, 5)
+    drain(meta2.at[0 : SIDE - 1], meta_recv.at[2])
+    drain(meta2.at[0 : 2 * SIDE - 2], meta_recv.at[4])
     for load in loads:
         load.wait()
     pre_t[...] = jnp.concatenate([pre_buf[0], pre_buf[1]], axis=1).astype(F32).T.astype(BF16)
@@ -320,97 +370,123 @@
         shares = jnp.sum(hid[hw, :, cols] * scores, axis=0, keepdims=True)
         part_send[hw, 2 * j] = shares[:, 0:128]
         part_send[hw, 2 * j + 1] = shares[:, 128:256]
-        d_gate = (gate_f[hw, :, cols] * scores).astype(BF16)
-        d_up = (up_f[hw, :, cols] * scores).astype(BF16)
+        score_buf[hw, :, cols] = scores
+
+    def share(w, j):
+        hw = source(w)
+        for px in (2 * j, 2 * j + 1):
+            for py in range(SIDE):
+                for core in range(2):
+                    own = (hw == h) & (px == x) & (py == y) & (core == k)
+
+                    @pl.when(own)
+                    def _():
+                        part_recv[me] = part_send[hw, px]
+
+                    @pl.when(jnp.logical_not(own))
+                    def _():
+                        remote(
+                            part_send.at[hw, px],
+                            part_recv.at[me],
+                            part_ssem.at[0],
+                            part_rsem.at[0],
+                            at(s, hw, core, px, py),
+                        ).start()
+
+    def grads_of(w):
+        hw = source(w)
+        d_gate = (gate_f[hw] * score_buf[hw]).astype(BF16)
+        d_up = (up_f[hw] * score_buf[hw]).astype(BF16)
         moved = lax.dot_general(
-            select[hw, :, cols], jnp.concatenate([d_gate, d_up], axis=0), NT, preferred_element_type=F32
+            select[hw], jnp.concatenate([d_gate, d_up], axis=0), NT, preferred_element_type=F32
         )
-        if j == 0:
-
-            @pl.when(w == 0)
-            def _():
-                slot_total[...] = moved
-
-            @pl.when(w > 0)
-            def _():
-                slot_total[...] += moved
-
-        else:
+
+        @pl.when(w == 0)
+        def _():
+            slot_total[...] = moved
+
+        @pl.when(w > 0)
+        def _():
             slot_total[...] += moved
 
-    def share(w):
-        hw = source(w)
-
-        @pl.loop(0, 8 * SIDE)
-        def _(j):
-            px, py, core = j // 8, lax.rem(j // 2, SIDE), lax.rem(j, 2)
-            own = (hw == h) & (px == x) & (py == y) & (core == k)
-
-            @pl.when(own)
-            def _():
-                part_recv[me] = part_send[hw, px]
-
-            @pl.when(jnp.logical_not(own))
-            def _():
-                remote(
-                    part_send.at[hw, px], part_recv.at[me], part_ssem.at[0], part_rsem.at[0], at(s, hw, core, px, py)
-                ).start()
-
-    def down_of(w, low, high, last):
-        hw = source(w)
-
-        @pl.loop(low, high)
+    def down_of(w, last):
+        hw, after = source(w), source(w + 1)
+        step = mid
+
+        @pl.loop(0, half // step)
         def _(c):
-            cols = pl.ds(pl.multiple_of(c * 512, 512), 512)
-            block = rows_buf[hw, :, :, :, :, cols].reshape(tokens, 512)
-            more = jnp.dot(scaled[hw], block, preferred_element_type=F32)
+            cols = pl.ds(pl.multiple_of(c * step, step), step)
+            block = jnp.concatenate(
+                [rows_buf[p, :, :, :, :, cols].reshape(tokens, step) for p in (hw, after)], axis=0
+            )
+            factor = jnp.concatenate([scaled[hw], scaled[after]], axis=1)
+            more = jnp.dot(factor, block, preferred_element_type=F32)
             if last:
                 down_buf[:, cols] = (total[:, cols] + more).astype(BF16)
             else:
-
-                @pl.when(w == 0)
-                def _():
-                    total[:, cols] = more
-
-                @pl.when(w > 0)
-                def _():
-                    total[:, cols] += more
-
-    tiles_of_down = half // 512
+                total[:, cols] = more
+
+    step4(0)
+    far_wait(0)
+    far_copy(rows_buf.at[h_first, x_far, y_far, k], 3, h_first, s, ring(h - 1)).start()
     prepare(0)
-    step4(0)
     z_wait(2)
-    step1(2)
+    step1(2, full)
 
     @pl.loop(1, SIDE)
     def _(w):
         step3(w)
+        step4(w)
         step5(w - 1)
 
         @pl.when(w < SIDE - 1)
         def _():
             step2(w + 1)
+
+        @pl.when(w == 1)
+        def _():
+            far_wait(1)
+            far_copy(rows_buf.at[source(1), x_far, y_far, k], 2, source(1), s, ring(h + 1)).start()
+
+        @pl.when(w == 2)
+        def _():
+            drain(meta2.at[0 : SIDE - 1], meta_recv.at[5])
+
+        @pl.when(w > 2)
+        def _():
+            far_wait(w - 1)
 
         prepare(w)
         arrived(w - 1)
         scores_of(w - 1, 0)
-        step4(w)
 
         @pl.when(w < SIDE - 2)
         def _():
             z_wait(w + 2)
-            step1(w + 2)
+            step1(w + 2, full)
 
         scores_of(w - 1, 1)
-        share(w - 1)
-        down_of(w - 1, 0, tiles_of_down, False)
-
+        share(w - 1, 0)
+        share(w - 1, 1)
+
+        @pl.when(w < SIDE - 1)
+        def _():
+            grads_of(w - 1)
+
+        @pl.when(w == 2)
+        def _():
+            down_of(0, False)
+
+    far_wait(SIDE - 1)
     step5(SIDE - 1)
     arrived(SIDE - 1)
     scores_of(SIDE - 1, 0)
+    share(SIDE - 1, 0)
     scores_of(SIDE - 1, 1)
-    share(SIDE - 1)
-    down_of(SIDE - 1, 0, tiles_of_down, True)
+    share(SIDE - 1, 1)
+    grads_of(SIDE - 2)
+    grads_of(SIDE - 1)
+    down_of(SIDE - 2, True)
     slot_out[0] = slot_total[:, 0:128].astype(BF16)
     slot_out[1] = slot_total[:, 128:256].astype(BF16)
 
@@ -418,7 +494,9 @@
     def _(w):
         sent(w)
         drain(rows_buf.at[0, 0, 0, 0], z_send.at[w])
-
+        drain(rows_buf.at[0, 0, 0, 0], far_send.at[w])
+
+    drain(own_buf, far_sem.at[0])
     drain(meta1.at[0 : 2 * SIDE - 1], meta_send.at[0])
     drain(meta2.at[0 : SIDE * SIDE - 1], meta_send.at[1])
 
@@ -478,6 +556,7 @@
         scratch_shapes=[
             pltpu.VMEM((SIDE, SIDE, SIDE, 2, ROWS, half), BF16),
             pltpu.VMEM((ROWS, half), BF16),
+            pltpu.VMEM((ROWS, half), BF16),
             pltpu.VMEM((2 * hidden, half), BF16),
             pltpu.VMEM((2, slots, hidden), BF16),
             pltpu.VMEM((2 * hidden, slots), BF16),
@@ -490,9 +569,10 @@
             pltpu.VMEM((SIDE, 2 * hidden, tokens), BF16),
             pltpu.VMEM((2 * hidden, half), F32),
             pltpu.VMEM((slots, 2 * hidden), F32),
+            pltpu.VMEM((SIDE, hidden, tokens), F32),
             pltpu.VMEM((SIDE, SIDE, 1, 128), F32),
             pltpu.VMEM((2 * SIDE * SIDE * SIDE, 1, 128), F32),
-            dma((SIDE,)),
+            dma((SIDE + 1,)),
             dma((SIDE, 4)),
             dma((SIDE, 2)),
             dma((SIDE, 4, 3)),
@@ -505,10 +585,13 @@
             dma((SIDE,)),
             dma((SIDE,)),
             dma((2,)),
-            dma((2,)),
+            dma((6,)),
             dma((1,)),
             dma((1,)),
             dma((4,)),
+            dma((2,)),
+            dma((SIDE,)),
+            dma((SIDE,)),
         ],
         compiler_params=pltpu.CompilerParams(
             collective_id=0, has_side_effects=True, vmem_limit_bytes=52 * 1024 * 1024

time: 86.2 us -> 82.4 us (0.956)
  the two profiles are of different devices: /device:TPU:64 before, /device:TPU:70 now
where the time goes in v4:
time: 82.4 us; the launch traced here: 82.2 us
  Pallas kernels  81.6 us (99%)
    pallas_call x1, Pallas kernels, shards(): pl.pallas_call(functools.partial(kernel, sections), out_shape=(pltpu.VMEM...  80.2 us

profile of v4, /device:TPU:70, one launch (start us, length us, event | category | flops | bytes accessed | tf_op | source)
XLA Modules:
  0.0 82.2 jit_solution(17402952933966554426)
XLA Ops:
  0.6 80.2 %shard_map.93 = (bf16[2,640,128]{2,1,0:T(8,128)(2,1)S(1)}, bf16[256,3584]{1,0:T(8,128)(2,1)S(1)}, f32[4,8]{1,0:T(4,128)S(1)}) custom-call(bf16[8,7168]{1,0:T(8,128)(2,1)} %bitcast.22, s32[4,8]{1,0:T(4,128)} %bitcast.23, bf16[4,8]{1,0:T(4,128)(2,1)} %bitcast.25, bf16[128,7168]{1,0:T(8,128)(2,1)} %bitcast.16, bf16[640,128]{1,0:T(8,128)(2,1)} %bitcast.18, ...), custom_call_target="tpu_custom_call" | custom-call | flops 2348810240 | bytes 3670016 | tf_op jit(solution)/shard_map/pallas_call | solution.py:547
  80.8 1.4 %shard_map.94 = (bf16[640,128]{1,0:T(8,128)(2,1)}, bf16[640,128]{1,0:T(8,128)(2,1)}, bf16[128,7168]{1,0:T(8,128)(2,1)}, f32[4,8]{1,0:T(4,128)}) custom-call(bf16[2,640,128]{2,1,0:T(8,128)(2,1)S(1)} %get-tuple-element.11.slot_in, bf16[256,3584]{1,0:T(8,128)(2,1)S(1)} %get-tuple-element.12.down_in, f32[4,8]{1,0:T(4,128)S(1)} %get-tuple-element.13.prob_in), custom_call_target="tpu_custom_call" | custom-call | tf_op jit(solution)/shard_map/pallas_call | solution.py:603

commit v5 on v4

--- a/solution.py
+++ b/solution.py
@@ -41,7 +41,6 @@
     gate_f,
     up_f,
     scaled,
-    total,
     slot_total,
     score_buf,
     part_send,
@@ -320,6 +319,9 @@
     z_wait(1)
     z_copy(rows_buf.at[source(1), x, y, k], 2, source(1), s, ring(h + 1)).start()
     step1(1, full)
+    for load in loads:
+        load.wait()
+    pre_t[...] = jnp.concatenate([pre_buf[0], pre_buf[1]], axis=1).astype(F32).T.astype(BF16)
 
     step3(0)
     step2(1)
@@ -327,9 +329,6 @@
     pass_on(across, 5)
     drain(meta2.at[0 : SIDE - 1], meta_recv.at[2])
     drain(meta2.at[0 : 2 * SIDE - 2], meta_recv.at[4])
-    for load in loads:
-        load.wait()
-    pre_t[...] = jnp.concatenate([pre_buf[0], pre_buf[1]], axis=1).astype(F32).T.astype(BF16)
     tokens = SIDE * 128
     slots = slot_total.shape[0]
 
@@ -409,22 +408,15 @@
         def _():
             slot_total[...] += moved
 
-    def down_of(w, last):
-        hw, after = source(w), source(w + 1)
-        step = mid
+    def down_all():
+        step = half // 4
+        factor = jnp.concatenate([scaled[p] for p in range(SIDE)], axis=1)
 
         @pl.loop(0, half // step)
         def _(c):
             cols = pl.ds(pl.multiple_of(c * step, step), step)
-            block = jnp.concatenate(
-                [rows_buf[p, :, :, :, :, cols].reshape(tokens, step) for p in (hw, after)], axis=0
-            )
-            factor = jnp.concatenate([scaled[hw], scaled[after]], axis=1)
-            more = jnp.dot(factor, block, preferred_element_type=F32)
-            if last:
-                down_buf[:, cols] = (total[:, cols] + more).astype(BF16)
-            else:
-                total[:, cols] = more
+            block = rows_buf[:, :, :, :, :, cols].reshape(SIDE * tokens, step)
+            down_buf[:, cols] = jnp.dot(factor, block, preferred_element_type=F32).astype(BF16)
 
     step4(0)
     far_wait(0)
@@ -472,10 +464,6 @@
         @pl.when(w < SIDE - 1)
         def _():
             grads_of(w - 1)
-
-        @pl.when(w == 2)
-        def _():
-            down_of(0, False)
 
     far_wait(SIDE - 1)
     step5(SIDE - 1)
@@ -486,7 +474,7 @@
     share(SIDE - 1, 1)
     grads_of(SIDE - 2)
     grads_of(SIDE - 1)
-    down_of(SIDE - 2, True)
+    down_all()
     slot_out[0] = slot_total[:, 0:128].astype(BF16)
     slot_out[1] = slot_total[:, 128:256].astype(BF16)
 
@@ -567,7 +555,6 @@
             pltpu.VMEM((SIDE, hidden, tokens), F32),
             pltpu.VMEM((SIDE, hidden, tokens), F32),
             pltpu.VMEM((SIDE, 2 * hidden, tokens), BF16),
-            pltpu.VMEM((2 * hidden, half), F32),
             pltpu.VMEM((slots, 2 * hidden), F32),
             pltpu.VMEM((SIDE, hidden, tokens), F32),
             pltpu.VMEM((SIDE, SIDE, 1, 128), F32),

time: 82.4 us -> 81 us (0.983)
  the two profiles are of different devices: /device:TPU:70 before, /device:TPU:64 now
where the time goes in v5:
time: 81 us; the launch traced here: 80.9 us
  Pallas kernels  80.2 us (99%)
    pallas_call x1, Pallas kernels, shards(): pl.pallas_call(functools.partial(kernel, sections), out_shape=(pltpu.VMEM...  78.9 us

profile of v5, /device:TPU:64, one launch (start us, length us, event | category | flops | bytes accessed | tf_op | source)
XLA Modules:
  0.0 80.9 jit_solution(4707064547712418738)
XLA Ops:
  0.6 78.9 %shard_map.93 = (bf16[2,640,128]{2,1,0:T(8,128)(2,1)S(1)}, bf16[256,3584]{1,0:T(8,128)(2,1)S(1)}, f32[4,8]{1,0:T(4,128)S(1)}) custom-call(bf16[8,7168]{1,0:T(8,128)(2,1)} %bitcast.22, s32[4,8]{1,0:T(4,128)} %bitcast.23, bf16[4,8]{1,0:T(4,128)(2,1)} %bitcast.25, bf16[128,7168]{1,0:T(8,128)(2,1)} %bitcast.16, bf16[640,128]{1,0:T(8,128)(2,1)} %bitcast.18, ...), custom_call_target="tpu_custom_call" | custom-call | flops 2348810240 | bytes 3670016 | tf_op jit(solution)/shard_map/pallas_call | solution.py:535
  79.5 1.4 %shard_map.94 = (bf16[640,128]{1,0:T(8,128)(2,1)}, bf16[640,128]{1,0:T(8,128)(2,1)}, bf16[128,7168]{1,0:T(8,128)(2,1)}, f32[4,8]{1,0:T(4,128)}) custom-call(bf16[2,640,128]{2,1,0:T(8,128)(2,1)S(1)} %get-tuple-element.11.slot_in, bf16[256,3584]{1,0:T(8,128)(2,1)S(1)} %get-tuple-element.12.down_in, f32[4,8]{1,0:T(4,128)S(1)} %get-tuple-element.13.prob_in), custom_call_target="tpu_custom_call" | custom-call | tf_op jit(solution)/shard_map/pallas_call | solution.py:590

commit v6 on v5

--- a/solution.py
+++ b/solution.py
@@ -461,10 +461,6 @@
         share(w - 1, 0)
         share(w - 1, 1)
 
-        @pl.when(w < SIDE - 1)
-        def _():
-            grads_of(w - 1)
-
     far_wait(SIDE - 1)
     step5(SIDE - 1)
     arrived(SIDE - 1)
@@ -472,8 +468,11 @@
     share(SIDE - 1, 0)
     scores_of(SIDE - 1, 1)
     share(SIDE - 1, 1)
-    grads_of(SIDE - 2)
-    grads_of(SIDE - 1)
+
+    @pl.loop(0, SIDE)
+    def _(w):
+        grads_of(w)
+
     down_all()
     slot_out[0] = slot_total[:, 0:128].astype(BF16)
     slot_out[1] = slot_total[:, 128:256].astype(BF16)

time: 81 us -> 82.2 us (1.015)
  Pallas kernels: 80.2 us -> 81.4 us
    pallas_call x1, Pallas kernels: 78.9 us -> 80.1 us  [shards(): pl.pallas_call(functools.partial(kernel, sections), out_shape=(pltpu.VMEM...]
where the time goes in v6:
time: 82.2 us; the launch traced here: 82.1 us
  Pallas kernels  81.4 us (99%)
    pallas_call x1, Pallas kernels, shards(): pl.pallas_call(functools.partial(kernel, sections), out_shape=(pltpu.VMEM...  80.1 us

profile of v6, /device:TPU:64, one launch (start us, length us, event | category | flops | bytes accessed | tf_op | source)
XLA Modules:
  0.0 82.1 jit_solution(7526734048916940241)
XLA Ops:
  0.6 80.1 %shard_map.93 = (bf16[2,640,128]{2,1,0:T(8,128)(2,1)S(1)}, bf16[256,3584]{1,0:T(8,128)(2,1)S(1)}, f32[4,8]{1,0:T(4,128)S(1)}) custom-call(bf16[8,7168]{1,0:T(8,128)(2,1)} %bitcast.22, s32[4,8]{1,0:T(4,128)} %bitcast.23, bf16[4,8]{1,0:T(4,128)(2,1)} %bitcast.25, bf16[128,7168]{1,0:T(8,128)(2,1)} %bitcast.16, bf16[640,128]{1,0:T(8,128)(2,1)} %bitcast.18, ...), custom_call_target="tpu_custom_call" | custom-call | flops 2348810240 | bytes 3670016 | tf_op jit(solution)/shard_map/pallas_call | solution.py:534
  80.7 1.4 %shard_map.94 = (bf16[640,128]{1,0:T(8,128)(2,1)}, bf16[640,128]{1,0:T(8,128)(2,1)}, bf16[128,7168]{1,0:T(8,128)(2,1)}, f32[4,8]{1,0:T(4,128)}) custom-call(bf16[2,640,128]{2,1,0:T(8,128)(2,1)S(1)} %get-tuple-element.11.slot_in, bf16[256,3584]{1,0:T(8,128)(2,1)S(1)} %get-tuple-element.12.down_in, f32[4,8]{1,0:T(4,128)S(1)} %get-tuple-element.13.prob_in), custom_call_target="tpu_custom_call" | custom-call | tf_op jit(solution)/shard_map/pallas_call | solution.py:589
